TPU v7x, 256 devices: a whole 4x4x8 slice. The times are simulated.
256 devices in a mesh: outer: 32 (over x, y, core), inner: 8 (over z).
Axes of the slice: x: 4, y: 4, z: 8, core: 2. Of those that a mesh axis runs over, the one named last changes fastest.
Arguments:
- tokens: bfloat16 [65536, 2048], P(('outer', 'inner')), may hold values from -6 to 6
- norm_gain: float32 [2048], replicated, may hold values from 0.25 to 1.75
- norm_bias: float32 [2048], replicated, may hold values from -3 to 3
- keep_mask: int32 [65536, 2048], P(('outer', 'inner')), may hold values 0 or 1
- projection: bfloat16 [3, 2048, 2048], P(None, 'outer', 'inner'), may hold values from -0.125 to 0.125
- head_gain: float32 [2048], P('inner'), may hold values from 0.25 to 1.75
- traj_starts: int32 [8], replicated, may hold values from 0 to 65535, as said below
Outputs:
- attended: bfloat16 [65536, 2048], P('outer', 'inner')
Inputs may be any that keep to these rules, and one draw needn't show every extreme that they name: `traj_starts`: 8 distinct positions in rising order, the first one 0 and the last one 65536 - 1; a trajectory runs from one entry to the next or to the row's end.
All inputs are finite; a program needn't handle non-finite values. No bound on the sum of `keep_mask` on one device may be relied on, other than what follows from the above.
Results may differ from a plain program's by a relative error of at most 0.0098.
Values may be sent and summed in bfloat16 or wider, within the bound.
A program may use at most 128 MiB of HBM per device.

v0:
```python
import jax
import jax.numpy as jnp
from jax import lax
from jax.sharding import PartitionSpec as P

HEAD_DIM = 128
SPAN = 512


def carried_in(value, axis, join, neutral):
    count, mine = (lax.axis_size(axis), lax.axis_index(axis))
    pieces = jax.tree.map(lambda part: lax.all_gather(part, axis), value)
    so_far = jax.tree.map(
        lambda part, zero: jnp.full_like(part, 0) + jnp.asarray(zero, part.dtype), value, neutral
    )

    def turn(position, so_far):
        longer = join(so_far, jax.tree.map(lambda part: part[position], pieces))
        return jax.tree.map(lambda new, old: jnp.where(position < mine, new, old), longer, so_far)

    return lax.fori_loop(0, count - 1, turn, so_far)


def segment_of(traj_starts, positions):
    hits = (traj_starts[None, :] <= positions[:, None]).astype(jnp.int32)
    return jnp.sum(hits, axis=1) - 1


def normalize(tokens, norm_gain, norm_bias, keep_mask):
    values = tokens.astype(jnp.float32)
    center = values - jnp.mean(values, axis=-1, keepdims=True)
    spread = jnp.mean(center * center, axis=-1, keepdims=True)
    scaled = (
        (center * lax.rsqrt(spread + 1e-05) * norm_gain + norm_bias)
        * keep_mask.astype(jnp.float32)
        / 0.9
    )
    return scaled.astype(jnp.bfloat16)


def span_step(carried, inputs_now):
    queries, keys_now, values_now, segment, before = inputs_now
    span_len = queries.shape[0]
    lower_mask = jnp.arange(span_len)[:, None] >= jnp.arange(span_len)[None, :]
    allowed = lower_mask & (segment[:, None] == segment[None, :])
    scores = jnp.einsum("thd,shd->hts", queries, keys_now, preferred_element_type=jnp.float32)
    rounded = jnp.where(allowed[None], scores, 0.0).astype(jnp.bfloat16)
    inside_term = jnp.einsum(
        "hts,shd->thd", rounded, values_now, preferred_element_type=jnp.float32
    )
    reach_mask = (segment == before).astype(jnp.float32)
    carried_term = jnp.einsum(
        "thd,hde->the", queries.astype(jnp.float32), carried, precision=lax.Precision.HIGHEST
    )
    mixed = inside_term + carried_term * reach_mask[:, None, None]
    last_seg = segment[-1]
    kept_values = jnp.where(
        (segment == last_seg)[:, None, None], values_now, jnp.zeros_like(values_now)
    )
    update = jnp.einsum("shd,she->hde", keys_now, kept_values, preferred_element_type=jnp.float32)
    carried = carried * (last_seg == before).astype(jnp.float32) + update
    return (carried, mixed)


def per_device(tokens, norm_gain, norm_bias, keep_mask, projection, head_gain, traj_starts):
    inner_count = lax.axis_size("inner")
    block_len = tokens.shape[0] * inner_count
    outer_index = lax.axis_index("outer")
    block_first = outer_index * block_len
    normed = normalize(tokens, norm_gain, norm_bias, keep_mask)
    row_weights = lax.all_gather(projection, "outer", axis=1, tiled=True)
    projected = jnp.einsum(
        "td,wdc->wtc",
        lax.all_gather(normed, "inner", axis=0, tiled=True),
        row_weights,
        preferred_element_type=jnp.float32,
    ).astype(jnp.bfloat16)
    local_width = projected.shape[2]
    head_count = local_width // HEAD_DIM
    queries = projected[0].reshape(block_len, head_count, HEAD_DIM)
    keys_all = projected[1].reshape(block_len, head_count, HEAD_DIM)
    values_all = projected[2].reshape(block_len, head_count, HEAD_DIM)
    positions = block_first + jnp.arange(block_len, dtype=jnp.int32)
    segment = segment_of(traj_starts, positions)
    span_count = block_len // SPAN
    span_firsts = block_first + jnp.arange(span_count, dtype=jnp.int32) * SPAN
    before = segment_of(traj_starts, span_firsts - 1)
    block_before = before[0]
    last_seg = segment[-1]
    tail_values = jnp.where(
        (segment == last_seg)[:, None, None], values_all, jnp.zeros_like(values_all)
    )
    block_state = jnp.einsum(
        "shd,she->hde", keys_all, tail_values, preferred_element_type=jnp.float32
    )
    resets = (last_seg != block_before).astype(jnp.float32)

    def combine(earlier, later):
        return (later[0] + earlier[0] * (1.0 - later[1]), jnp.maximum(earlier[1], later[1]))

    empty = (jnp.zeros_like(block_state), jnp.zeros((), jnp.float32))
    incoming, unused = carried_in((block_state, resets), "outer", combine, empty)
    stacked = (
        queries.reshape(span_count, SPAN, head_count, HEAD_DIM),
        keys_all.reshape(span_count, SPAN, head_count, HEAD_DIM),
        values_all.reshape(span_count, SPAN, head_count, HEAD_DIM),
        segment.reshape(span_count, SPAN),
        before,
    )
    unused_state, mixed = lax.scan(span_step, incoming, stacked)
    mixed = mixed.reshape(block_len, head_count, HEAD_DIM)
    scale_back = lax.rsqrt(jnp.mean(mixed * mixed, axis=-1, keepdims=True) + 1e-06)
    return ((mixed * scale_back).reshape(block_len, local_width) * head_gain).astype(jnp.bfloat16)


def solution(mesh):
    placed = (
        P(("outer", "inner"), None),
        P(),
        P(),
        P(("outer", "inner"), None),
        P(None, "outer", "inner"),
        P("inner"),
        P(),
    )
    return jax.shard_map(
        per_device, mesh=mesh, in_specs=placed, out_specs=P("outer", "inner"), check_vma=False
    )
```

profile of v0, /device:TPU:1, one launch (start us, length us, event | category | flops | bytes accessed | tf_op | source)
XLA Modules:
  0.0 373.3 jit_solution(9047212150586259808)
XLA Ops:
  7.3 1.4 convert_reduce_fusion
  8.8 1.6 fusion.43
  10.5 3.3 fusion.48
  15.1 49.3 %all-gather.7.cloned.1.call-done = bf16[3,2048,256]{2,1,0:T(8,128)(2,1)} async-done(((bf16[3,64,256]{2,1,0:T(8,128)(2,1)}), bf16[3,2048,256]{2,1,0:T(8,128)(2,1)}) %all-gather.7.cloned.1.call-update) | async-done | bytes 3145744 | tf_op jit(solution)/shard_map/all_gather | solution.py:71
  64.4 95.0 %all-gather.5.cloned.1.call-done = bf16[2048,2048]{1,0:T(8,128)(2,1)} async-done(((bf16[256,2048]{1,0:T(8,128)(2,1)}), bf16[2048,2048]{1,0:T(8,128)(2,1)}) %all-gather.5.cloned.1.call-update) | async-done | bytes 8388624 | tf_op jit(solution)/shard_map/all_gather | solution.py:74
  159.3 10.1 %fusion.38 = bf16[3,2048,256]{1,2,0:T(8,128)(2,1)S(1)} fusion(bf16[3,2048,256]{2,1,0:T(8,128)(2,1)} %all-gather.7.cloned.1.call-done, bf16[2048,2048]{1,0:T(8,128)(2,1)} %all-gather.5.cloned.1.call-done), kind=kOutput, calls=%fused_computation.40 | convolution fusion | flops 6444023808 | bytes 14680064 | tf_op jit(solution)/shard_map/td,wdc->wtc/dot_general | solution.py:72
  174.8 63.1 %all-reduce = f32[32]{0:T(128)S(1)} all-reduce(f32[32]{0:T(128)S(1)} %dynamic-update-slice), channel_id=1, replica_groups=mesh['outer'=32,'inner'=8] {'outer'}, use_global_device_ids=true, to_apply=%add | all-reduce | flops 32 | bytes 256
  237.9 2.6 reshape_reshape_squeeze.9
  240.5 1.6 reshape_reshape_squeeze.10
  242.1 2.5 copy.35
  245.8 1.8 reshape_reshape_squeeze.11
  247.7 1.7 copy.37
  249.4 73.4 %while.27 = (s32[]{:T(128)}, f32[2,128,128]{2,1,0:T(8,128)S(1)}, s32[]{:T(128)}, f32[32,2,128,128]{3,2,1,0:T(8,128)}, f32[32]{0:T(128)S(1)}, /*index=5*/s32[]{:T(128)}, f32[1]{0:T(128)}, s32[]{:T(128)}) while((s32[]{:T(128)}, f32[2,128,128]{2,1,0:T(8,128)S(1)}, s32[]{:T(128)}, f32[32,2,128,128]{3,2,1,0:T(8,128)}, f32[32]{0:T(128)S(1)}, ...), condition=%wide.region_5.6_spmd.clone, body=%wide.region_4.5_spmd.clone.sunk | while | flops 131077 | bytes 393353 | solution.py:21
  322.7 34.8 %while.26 = (s32[]{:T(128)}, f32[2,128,128]{2,1,0:T(8,128)S(1)}, f32[4,512,2,128]{1,3,2,0:T(8,128)S(1)}, s32[4,512]{1,0:T(4,128)S(1)}, s32[4]{0:T(128)S(1)}, /*i...) while((s32[]{:T(128)}, f32[2,128,128]{2,1,0:T(8,128)S(1)}, ...), condition=%wide.region_7.8_spmd, body=%wide.region_6.7_spmd.sunk | while | flops 505611776 | bytes 4080303 | solution.py:110
  325.4 1.4 fusion.76
  327.0 1.8 fusion.78
  334.1 1.4 fusion.76
  335.7 1.8 fusion.78
  342.8 1.4 fusion.76
  344.4 1.8 fusion.78
  353.1 1.8 fusion.78
  357.8 2.3 copy.38
  360.6 4.7 %mul.95 = f32[2048,2,128]{2,1,0:T(2,128)S(1)} broadcast(f32[2048,2]{1,0:T(8,128)S(1)} %copy.39), dimensions={0,1} | broadcast | bytes 2113536 | tf_op jit(solution)/shard_map/mul | solution.py:113
  365.3 1.5 fusion.50
  (135 shorter events, 77.6 us)
Async XLA Ops:
  6.5 3.9 %copy-start = (bf16[256,2048]{1,0:T(8,128)(2,1)S(1)}, bf16[256,2048]{1,0:T(8,128)(2,1)}, u32[]{:S(2)}) copy-start(bf16[256,2048]{1,0:T(8,128)(2,1)} %param.11) | copy-start | bytes 3145732
  6.5 3.9 %copy-start.5 = (f32[2048]{0:T(1024)S(1)}, f32[2048]{0:T(1024)}, u32[]{:S(2)}) copy-start(f32[2048]{0:T(1024)} %param.12) | copy-start | bytes 24580
  6.5 3.9 %copy-start.4 = (f32[2048]{0:T(1024)S(1)}, f32[2048]{0:T(1024)}, u32[]{:S(2)}) copy-start(f32[2048]{0:T(1024)} %param.13) | copy-start | bytes 24580
  6.5 57.8 %all-gather.7.cloned.1.call-start = ((), (), s32[]{:S(2)}) async-start(), calls=%async_computation.1 | async-start | bytes 3244032 | tf_op jit(solution)/shard_map/all_gather | solution.py:71
  7.3 152.1 %all-gather.5.cloned.1.call-start = ((), (), s32[]{:S(2)}) async-start(), calls=%async_computation | async-start | bytes 9437184 | tf_op jit(solution)/shard_map/all_gather | solution.py:74
  10.4 3.4 copy-start.7
  13.7 235.6 %all-gather.9.cloned.1.call-start = ((), (), s32[]{:S(2)}) async-start(), calls=%async_computation.2 | async-start | bytes 4325376 | tf_op jit(solution)/shard_map/all_gather | solution.py:12
  170.7 2.0 copy-start.3
  171.3 2.2 copy-start.8
  242.1 2.5 copy-start.2
  360.2 5.1 %copy-start.1 = (f32[4,512,2,128]{3,2,1,0:T(2,128)S(1)}, f32[4,512,2,128]{3,2,1,0:T(2,128)}, u32[]{:S(2)}) copy-start(f32[4,512,2,128]{3,2,1,0:T(2,128)} %copy.38) | copy-start | bytes 6291460
  360.2 5.1 %copy-start.6 = (f32[256]{0:T(256)S(1)}, f32[256]{0:T(256)}, u32[]{:S(2)}) copy-start(f32[256]{0:T(256)} %param.16) | copy-start | bytes 3076
Sparse Core Ops, SparseCore 0:
  10.0 54.3 all-gather.6
  66.2 93.1 all-gather.4
  172.8 50.1 all-gather.8
where the time goes:
time: 377 us; the launch traced here: 373 us
  waiting for transfers between devices  145 us (38%)
  blocking collectives  63.1 us (17%)
  local copies, waits for them, and re-layouts  48.4 us (13%)
  other arithmetic  45.6 us (12%)
  matrix products  29.4 us (8%)
  loops' own time  27.7 us (7%)
  between operations  13.9 us (4%)
    all_gather x1, waiting for transfers between devices, per_device(): lax.all_gather(normed, 'inner', axis=0, tiled=True)  95 us
    unnamed x1, blocking collectives  63.1 us
    all_gather x1, waiting for transfers between devices, per_device(): row_weights = lax.all_gather(projection, 'outer', axis=1, tiled=True)  49.3 us
    select_n x31, other arithmetic, turn(): jnp.where(position < mine, new, old)  30.5 us
    another operation x1, loops' own time, carried_in(): return lax.fori_loop(0, count - 1, turn, so_far)  22.3 us
    dynamic_slice x31, local copies, waits for them, and re-layouts, turn(): longer = join(so_far, jax.tree.map(lambda part: part[position], pieces))  20.6 us
    dot_general x1, matrix products, per_device(): jnp.einsum('td,wdc->wtc', lax.all_gather(normed, 'inner', axis=0, tiled=T...  10.1 us
    while x4, local copies, waits for them, and re-layouts, per_device(): unused_state, mixed = lax.scan(span_step, incoming, stacked)  7.73 us
  transfers between devices with their start and end apart: 3, of which 2 were waited for; matrix products, arithmetic and copies ran while one was open for 5% of the time, Pallas kernels for 0%

commit v1 on v0

v1 whole, which is shorter than its diff:
```python
import jax
import jax.numpy as jnp
from jax import lax
from jax.experimental import pallas as pl
from jax.experimental.pallas import tpu as pltpu
from jax.sharding import PartitionSpec as P

MESH = pl.DeviceIdType.MESH
F32, BF16, I32 = jnp.float32, jnp.bfloat16, jnp.int32
D, HEAD, SPAN = 2048, 128, 512
OWN = 256
PARTS = 4
PART = OWN // PARTS
RANGES = ((1, 2), (0, 1))
UNITS = ((0, 0), (1, 0), (0, 1), (1, 1))


def slot_of(dist):
    return 1 - dist // 2


def core_of(dist):
    return ((dist + 1) // 2) % 2


def plane_at(head_plane, dist):
    up = (head_plane + dist) % 8
    down = (head_plane + 8 - dist) % 8
    return jnp.where(up % 2 == 0, up, down)


def kernel(
    tok_hbm, gain, bias, mask_hbm, proj_hbm, head_gain, traj, out,
    tok, mask, x_all, w_all, qkv, inside, a_out, rz, local_c, t_all, tp, ps, p_all, c_out, cr, gains, outs,
    in_sem, wz_send, wz_recv, ring_send, ring_recv, tok_send, tok_recv, fwd_send, sib_recv, hg_send, hg_recv,
    rz_send, rz_recv, a2a_send, a2a_recv, cr_send, cr_recv, out_send, out_recv,
):
    outer, z = lax.axis_index("outer"), lax.axis_index("inner")
    core, chip = outer % 2, outer // 2
    cx, cy = chip // 4, chip % 4
    pair, member = z // 2, z % 2
    along = jnp.where(core == 0, cx, cy)
    across = jnp.where(core == 0, cy, cx)

    def chip_at(a, b):
        return a * (4 - 3 * core) + b * (1 + 3 * core)

    a_next, a_prev = (along + 1) % 4, (along + 3) % 4
    b_next, b_prev = (across + 1) % 4, (across + 3) % 4

    def plane_dev(chip_id):
        return (chip_id * 2 + core, z)

    def column_dev(core_id, plane):
        return (chip * 2 + core_id, plane)

    dists = (3 - core, core)
    step = 2 * member - 1
    planes = tuple((z + step * d + 8) % 8 for d in dists)

    def remote(src, dst, send, recv, device):
        return pltpu.make_async_remote_copy(
            src_ref=src, dst_ref=dst, send_sem=send, recv_sem=recv, device_id=device, device_id_type=MESH
        )

    def wait_for(ref, sem):
        pltpu.make_async_copy(ref, ref, sem).wait()

    def in_copies(i):
        rows = pl.ds(i * PART, PART)
        return (
            pltpu.make_async_copy(tok_hbm.at[rows], tok.at[rows], in_sem.at[0, i]),
            pltpu.make_async_copy(mask_hbm.at[rows], mask.at[rows], in_sem.at[1, i]),
        )

    for i in range(PARTS):
        for copy in in_copies(i):
            copy.start()

    barrier = pltpu.get_barrier_semaphore()

    def greet_plane(i, carry):
        pl.semaphore_signal(barrier, inc=1, device_id=plane_dev((chip + i) % 16), device_id_type=MESH)
        return carry

    def greet_column(i, carry):
        spot = (z * 2 + core + i) % 16
        pl.semaphore_signal(barrier, inc=1, device_id=column_dev(spot % 2, spot // 2), device_id_type=MESH)
        return carry

    lax.fori_loop(1, 16, greet_column, 0)
    lax.fori_loop(1, 16, greet_plane, 0)
    pl.semaphore_wait(barrier, 30)

    def wz_copy(d, r):
        first, count = RANGES[r]
        src = proj_hbm.at[pl.ds(first, count)]
        dst = w_all.at[slot_of(d), pl.ds(first, count), cx, cy, pl.ds(core * 64, 64)]
        return src, dst, wz_send.at[d, r], wz_recv.at[slot_of(d), r, core], column_dev(core_of(d), plane_at(z, d))

    for r in range(2):
        for d in (3, 2, 1, 0):
            src, dst, send, recv, device = wz_copy(d, r)
            if d == 0:

                @pl.when(core == 0)
                def _():
                    pltpu.make_async_copy(src, dst, recv).start()

                @pl.when(core == 1)
                def _():
                    remote(src, dst, send, recv, device).start()

            else:
                remote(src, dst, send, recv, device).start()
    for d in range(4):

        @pl.when((core == core_of(d)) if d else (core == 2))
        def _():
            s = slot_of(d)
            remote(head_gain, gains.at[s], hg_send.at[s], hg_recv.at[s], column_dev(core, plane_at(z, d))).start()

    @pl.when(core == 0)
    def _():
        gains[1] = head_gain[...]

    def wait_wz(u):
        s, r = UNITS[u]
        first, count = RANGES[r]
        for half in range(2):
            wait_for(w_all.at[s, pl.ds(first, count), 0, 0, pl.ds(half * 64, 64)], wz_recv.at[s, r, half])

    def block(u, chip_id, rows=None):
        s, r = UNITS[u]
        first, count = RANGES[r]
        ref = w_all.at[s, pl.ds(first, count), chip_id // 4, chip_id % 4]
        return ref if rows is None else ref.at[:, pl.ds(rows, 64)]

    def line_x(u, b, rows=None):
        s, r = UNITS[u]
        first, count = RANGES[r]
        ref = w_all.at[s, pl.ds(first, count), :, b]
        return ref if rows is None else ref.at[:, :, pl.ds(rows, 64)]

    def line_y(u, b, rows=None):
        s, r = UNITS[u]
        first, count = RANGES[r]
        ref = w_all.at[s, pl.ds(first, count), b]
        return ref if rows is None else ref.at[:, :, pl.ds(rows, 64)]

    def ring_sems(u, stage, way):
        return ring_send.at[u, stage, way], ring_recv.at[u, stage, way]

    a_devices = (plane_dev(chip_at(a_next, across)), plane_dev(chip_at(a_prev, across)))
    b_devices = (plane_dev(chip_at(along, b_next)), plane_dev(chip_at(along, b_prev)))

    def a1(u):
        wait_wz(u)
        for way in range(2):
            ref = block(u, chip)
            remote(ref, ref, *ring_sems(u, 0, way), a_devices[way]).start()

    def wait_ring(u, stage):
        for way in range(2):
            ref = line_y(u, 0, 64 * way if stage == 3 else None) if stage >= 2 else block(u, 0, 64 * way if stage == 1 else None)
            wait_for(ref, ring_recv.at[u, stage, way])

    def a2(u):
        wait_ring(u, 0)
        for way in range(2):
            ref = block(u, chip_at(a_prev if way == 0 else a_next, across), 64 * way)
            remote(ref, ref, *ring_sems(u, 1, way), a_devices[way]).start()

    def b_send(u, stage, spots, halves):
        @pl.when(core == 0)
        def _():
            for way in range(2):
                ref = line_x(u, spots[way], 64 * way if halves else None)
                remote(ref, ref, *ring_sems(u, stage, way), b_devices[way]).start()

        @pl.when(core == 1)
        def _():
            for way in range(2):
                ref = line_y(u, spots[way], 64 * way if halves else None)
                remote(ref, ref, *ring_sems(u, stage, way), b_devices[way]).start()

    def b1(u):
        wait_ring(u, 1)
        b_send(u, 2, (across, across), False)

    def b2(u):
        wait_ring(u, 2)
        b_send(u, 3, (b_prev, b_next), True)

    def b_done(u):
        wait_ring(u, 3)

    def ring_wait_sends(u):
        for stage in range(4):
            for way in range(2):
                half = 64 * way if stage in (1, 3) else None
                ref = line_y(u, 0, half) if stage >= 2 else block(u, 0, half)
                wait_for(ref, ring_send.at[u, stage, way])

    partner = column_dev(core, z + 1 - 2 * member)
    sibling = column_dev(1 - core, z)

    def token_rows(c, m, i):
        return x_all.at[c, m, pl.ds(i * PART, PART)]

    def normalize(i):
        for copy in in_copies(i):
            copy.wait()

        def rows16(j, carry):
            rows = pl.ds(pl.multiple_of(i * PART + j * 16, 16), 16)
            values = tok[rows, :].astype(F32)
            center = values - jnp.mean(values, axis=-1, keepdims=True)
            spread = jnp.mean(center * center, axis=-1, keepdims=True)
            scaled = center * lax.rsqrt(spread + 1e-05) * gain[...] + bias[...]
            x_all[core, member, rows, :] = (scaled * (mask[rows, :].astype(F32) * (1.0 / 0.9))).astype(BF16)
            return carry

        lax.fori_loop(0, PART // 16, rows16, 0)

    def send_tokens(i):
        ref = token_rows(core, member, i)
        remote(ref, ref, tok_send.at[0, i], tok_recv.at[i], partner).start()
        remote(ref, ref, tok_send.at[1, i], sib_recv.at[0, i], sibling).start()

    def forward_tokens(i):
        ref = token_rows(core, 1 - member, i)
        wait_for(ref, tok_recv.at[i])
        remote(ref, ref, fwd_send.at[i], sib_recv.at[1, i], sibling).start()

    def project(s, w, m):
        weights = w_all.at[s, w]

        def rows256(c, carry):
            product = jnp.dot(x_all[c, m], weights[...].reshape(D, 256), preferred_element_type=F32)
            rows = pl.ds(pl.multiple_of(m * OWN, OWN), OWN)
            qkv[s, w, c, rows, :] = product.astype(BF16)
            return carry

        lax.fori_loop(0, 2, rows256, 0)

    def start_of(position):
        first = jnp.full_like(position, -1)
        for i in range(8):
            first = jnp.where(traj[i] <= position, traj[i], first)
        return first

    def keeps(first, length):
        return jnp.where(start_of(first + (length - 1)) < first, 1.0, 0.0).astype(F32)

    chip_first = chip * 8 * SPAN

    def span_first(c):
        return chip_first + (c * 4 + pair) * SPAN

    def states(s):
        def one_span(c, carry):
            first = span_first(c)
            last_start = start_of(first + (SPAN - 1))
            spots = first + lax.broadcasted_iota(I32, (SPAN, HEAD), 0)
            kept = spots >= last_start
            for h in range(2):
                columns = slice(h * HEAD, (h + 1) * HEAD)
                values = jnp.where(kept, qkv[s, 2, c, :, columns].astype(F32), 0.0).astype(BF16)
                state = lax.dot_general(
                    qkv[s, 1, c, :, columns], values, (((0,), (0,)), ((), ())), preferred_element_type=F32
                )
                a_out[s, c, columns, :] = state.astype(BF16)
            return carry

        lax.fori_loop(0, 2, one_span, 0)

    def send_states(s):
        mine = dists[s]
        for i in range(1, 4):
            other = (mine + i) % 4
            remote(
                a_out.at[s, :, pl.ds(pl.multiple_of(other * 64, 64), 64)], rz.at[slot_of(other), :, pair],
                rz_send.at[s, i - 1], rz_recv.at[slot_of(other), pair],
                column_dev(core_of(other), plane_at(planes[s], other)),
            ).start()
        rz[s, :, pair] = a_out[s, :, pl.ds(pl.multiple_of(mine * 64, 64), 64), :]

    def wait_states(s):
        for i in range(1, 4):
            spot = (pair + i) % 4
            wait_for(rz.at[s, :, spot], rz_recv.at[s, spot])

    def chip_totals():
        for s in range(2):
            total = jnp.zeros((64, HEAD), F32)
            for j in range(8):
                local_c[j, s] = total
                total = total * keeps(chip_first + j * SPAN, SPAN) + rz[s, j // 4, j % 4].astype(F32)
            t_all[s * 64:(s + 1) * 64, :] = total

        def send(i, carry):
            other = (chip + i) % 16
            remote(
                t_all.at[pl.ds(pl.multiple_of(other * 8, 8), 8)], tp.at[chip], a2a_send.at[0], a2a_recv.at[0],
                plane_dev(other),
            ).start()
            return carry

        lax.fori_loop(1, 16, send, 0)
        tp[chip] = t_all[pl.ds(pl.multiple_of(chip * 8, 8), 8), :]

    def prefixes():
        wait_for(tp.at[pl.ds(0, 15)], a2a_recv.at[0])
        total = jnp.zeros((8, HEAD), F32)
        for k in range(16):
            ps[k] = total
            if k < 15:
                total = total * keeps(k * 8 * SPAN, 8 * SPAN) + tp[k]

        def send(i, carry):
            other = (chip + i) % 16
            remote(
                ps.at[other], p_all.at[pl.ds(pl.multiple_of(chip * 8, 8), 8)], a2a_send.at[1], a2a_recv.at[1],
                plane_dev(other),
            ).start()
            return carry

        lax.fori_loop(1, 16, send, 0)
        p_all[pl.ds(pl.multiple_of(chip * 8, 8), 8), :] = ps[chip]

    def carried():
        wait_for(tp.at[pl.ds(0, 15)], a2a_recv.at[1])
        reach = jnp.ones((), F32)
        for j in range(8):
            for s in range(2):
                total = local_c[j, s] + p_all[s * 64:(s + 1) * 64, :] * reach
                c_out[s, j // 4, j % 4] = total.astype(BF16)
            reach = reach * keeps(chip_first + j * SPAN, SPAN)
        for s in range(2):
            mine = dists[s]
            rows = pl.ds(pl.multiple_of(mine * 64, 64), 64)
            for i in range(1, 4):
                other = (mine + i) % 4
                plane = plane_at(planes[s], other)
                remote(
                    c_out.at[s, :, plane // 2], cr.at[slot_of(other), :, rows],
                    cr_send.at[s, i - 1], cr_recv.at[slot_of(other), mine],
                    column_dev(core_of(other), plane),
                ).start()
            cr[s, :, rows, :] = c_out[s, :, pair]

    def wait_carried(s):
        for i in range(1, 4):
            spot = (dists[s] + i) % 4
            wait_for(cr.at[s, :, pl.ds(0, 64)], cr_recv.at[s, spot])

    def inside_terms(s):
        def one_span(c, carry):
            first = span_first(c)
            for top in (0, 256):
                span_keys = top + 256
                rows = first + top + lax.broadcasted_iota(I32, (256, 1), 0)
                spots = first + lax.broadcasted_iota(I32, (256, span_keys), 1)
                allowed = (spots <= rows) & (spots >= start_of(rows))
                for h in range(2):
                    columns = slice(h * HEAD, (h + 1) * HEAD)
                    scores = lax.dot_general(
                        qkv[s, 0, c, top:top + 256, columns], qkv[s, 1, c, :span_keys, columns],
                        (((1,), (1,)), ((), ())), preferred_element_type=F32,
                    )
                    rounded = jnp.where(allowed, scores, 0.0).astype(BF16)
                    inside[s, c, top:top + 256, columns] = jnp.dot(
                        rounded, qkv[s, 2, c, :span_keys, columns], preferred_element_type=F32
                    )
            return carry

        lax.fori_loop(0, 2, one_span, 0)

    def finish(s):
        def one_span(c, carry):
            first = span_first(c)
            rows = first + lax.broadcasted_iota(I32, (SPAN, 1), 0)
            reached = start_of(rows) < first
            for h in range(2):
                columns = slice(h * HEAD, (h + 1) * HEAD)
                term = jnp.dot(qkv[s, 0, c, :, columns], cr[s, c, columns, :], preferred_element_type=F32)
                mixed = inside[s, c, :, columns] + jnp.where(reached, term, 0.0)
                scale_back = lax.rsqrt(jnp.mean(mixed * mixed, axis=-1, keepdims=True) + 1e-06)
                outs[s, c, :, columns] = (mixed * scale_back * gains[s, 0:1, columns]).astype(BF16)
            return carry

        lax.fori_loop(0, 2, one_span, 0)

    def send_out(s):
        rows = pl.ds(pl.multiple_of(pair * SPAN, SPAN), SPAN)
        for c in range(2):
            device = column_dev(c, planes[s])
            args = (outs.at[s, c], out.at[rows])
            if s == 1 and c == 0:

                @pl.when(core == 0)
                def _():
                    pltpu.make_async_copy(*args, out_recv.at[pair]).start()

                @pl.when(core == 1)
                def _():
                    remote(*args, out_send.at[s, c], out_recv.at[pair], device).start()

            else:
                remote(*args, out_send.at[s, c], out_recv.at[pair], device).start()

    normalize(0)
    send_tokens(0)
    a1(0)
    normalize(1)
    send_tokens(1)
    a1(1)
    normalize(2)
    send_tokens(2)
    a2(0)
    normalize(3)
    send_tokens(3)
    b1(0)
    a2(1)
    b1(1)
    a1(2)
    a1(3)
    forward_tokens(0)
    forward_tokens(1)
    b2(0)
    a2(2)
    a2(3)
    b_done(0)
    for i in range(PARTS):
        wait_for(token_rows(1 - core, member, i), sib_recv.at[0, i])
    for w in (1, 2):
        project(0, w, member)
    forward_tokens(2)
    b2(1)
    b1(2)
    forward_tokens(3)
    b1(3)
    b_done(1)
    for w in (1, 2):
        project(1, w, member)
    for i in range(PARTS):
        wait_for(token_rows(1 - core, 1 - member, i), sib_recv.at[1, i])
    for s in range(2):
        for w in (1, 2):
            project(s, w, 1 - member)
        states(s)
        send_states(s)
    b2(2)
    b_done(2)
    for s in range(2):
        wait_states(s)
    chip_totals()
    for m in range(2):
        project(0, 0, m)
    b2(3)
    prefixes()
    inside_terms(0)
    carried()
    b_done(3)
    for m in range(2):
        project(1, 0, m)
    inside_terms(1)
    wait_carried(0)

    @pl.when(core == 0)
    def _():
        wait_for(gains.at[0], hg_recv.at[0])

    @pl.when(core == 1)
    def _():
        for s in range(2):
            wait_for(gains.at[s], hg_recv.at[s])

    finish(0)
    send_out(0)
    wait_carried(1)
    finish(1)
    send_out(1)

    for r in range(2):
        first, count = RANGES[r]
        ref = w_all.at[0, pl.ds(first, count), 0, 0, pl.ds(0, 64)]
        for d in (1, 2, 3):
            wait_for(ref, wz_send.at[d, r])

        @pl.when(core == 1)
        def _():
            wait_for(ref, wz_send.at[0, r])

    @pl.when(core == 0)
    def _():
        wait_for(gains.at[0], hg_send.at[0])

    @pl.when(core == 1)
    def _():
        for s in range(2):
            wait_for(gains.at[s], hg_send.at[s])

    for u in range(4):
        ring_wait_sends(u)
    for i in range(PARTS):
        ref = token_rows(0, 0, i)
        for sem in (tok_send.at[0, i], tok_send.at[1, i], fwd_send.at[i]):
            wait_for(ref, sem)
    for s in range(2):
        for i in range(3):
            wait_for(rz.at[s, :, 0], rz_send.at[s, i])
            wait_for(rz.at[s, :, 0], cr_send.at[s, i])
    for i in range(2):
        wait_for(tp.at[pl.ds(0, 15)], a2a_send.at[i])
    for s in range(2):
        for c in range(2):
            if s == 1 and c == 0:

                @pl.when(core == 1)
                def _():
                    wait_for(outs.at[s, c], out_send.at[s, c])

            else:
                wait_for(outs.at[s, c], out_send.at[s, c])
    for p in range(4):
        wait_for(outs.at[0, 0], out_recv.at[p])


def per_device(tokens, norm_gain, norm_bias, keep_mask, projection, head_gain, traj_starts):
    any_spec = pl.BlockSpec(memory_space=pl.ANY)
    vmem = pl.BlockSpec(memory_space=pltpu.VMEM)
    dma = pltpu.SemaphoreType.DMA
    return pl.pallas_call(
        kernel,
        out_shape=jax.ShapeDtypeStruct((2048, 256), BF16),
        in_specs=[any_spec, vmem, vmem, any_spec, any_spec, vmem, pl.BlockSpec(memory_space=pltpu.SMEM)],
        out_specs=vmem,
        scratch_shapes=[
            pltpu.VMEM((OWN, D), BF16),
            pltpu.VMEM((OWN, D), I32),
            pltpu.VMEM((2, 2, OWN, D), BF16),
            pltpu.VMEM((2, 3, 4, 4, 128, 256), BF16),
            pltpu.VMEM((2, 3, 2, SPAN, 256), BF16),
            pltpu.VMEM((2, 2, SPAN, 256), F32),
            pltpu.VMEM((2, 2, 256, HEAD), BF16),
            pltpu.VMEM((2, 2, 4, 64, HEAD), BF16),
            pltpu.VMEM((8, 2, 64, HEAD), F32),
            pltpu.VMEM((128, HEAD), F32),
            pltpu.VMEM((16, 8, HEAD), F32),
            pltpu.VMEM((16, 8, HEAD), F32),
            pltpu.VMEM((128, HEAD), F32),
            pltpu.VMEM((2, 2, 4, 64, HEAD), BF16),
            pltpu.VMEM((2, 2, 256, HEAD), BF16),
            pltpu.VMEM((2, 8, 256), F32),
            pltpu.VMEM((2, 2, SPAN, 256), BF16),
            dma((2, PARTS)),
            dma((4, 2)),
            dma((2, 2, 2)),
            dma((4, 4, 2)),
            dma((4, 4, 2)),
            dma((2, PARTS)),
            dma((PARTS,)),
            dma((PARTS,)),
            dma((2, PARTS)),
            dma((2,)),
            dma((2,)),
            dma((2, 3)),
            dma((2, 4)),
            dma((2,)),
            dma((2,)),
            dma((2, 3)),
            dma((2, 4)),
            dma((2, 2)),
            dma((4,)),
        ],
        compiler_params=pltpu.CompilerParams(
            collective_id=0, has_side_effects=True, vmem_limit_bytes=48 * 1024 * 1024
        ),
    )(
        tokens, norm_gain.reshape(1, D), norm_bias.reshape(1, D), keep_mask, projection,
        jnp.broadcast_to(head_gain[None, :], (8, 256)), traj_starts,
    )


def solution(mesh):
    placed = (
        P(("outer", "inner"), None),
        P(),
        P(),
        P(("outer", "inner"), None),
        P(None, "outer", "inner"),
        P("inner"),
        P(),
    )
    return jax.shard_map(
        per_device, mesh=mesh, in_specs=placed, out_specs=P("outer", "inner"), check_vma=False
    )
```

time: 377 us -> 117 us (0.31)
  waiting for transfers between devices: 145 us -> 0 us
  Pallas kernels: 0 us -> 109 us
  blocking collectives: 63.1 us -> 0 us
  other arithmetic: 45.6 us -> 0 us
  local copies, waits for them, and re-layouts: 48.4 us -> 7.41 us
  matrix products: 29.4 us -> 0 us
  loops' own time: 27.7 us -> 0 us
  between operations: 13.9 us -> 0.02 us
    all_gather x3 -> x0, waiting for transfers between devices: 144 us -> none  [the longest x1 95 us: per_device(): lax.all_gather(normed, 'inner', axis=0, tiled=True)]
    pallas_call x0 -> x1, Pallas kernels: none -> 109 us  [per_device(): pl.pallas_call(kernel, out_shape=jax.ShapeDtypeStruct((2048, 256), BF16),...]
    unnamed x1 -> x0, blocking collectives: 63.1 us -> none
    select_n x31 -> x0, other arithmetic: 30.5 us -> none  [turn(): jnp.where(position < mine, new, old)]
    dot_general x14 -> x0, matrix products: 29.4 us -> none  [the longest x1 10.1 us: per_device(): jnp.einsum('td,wdc->wtc', lax.all_gather(normed, 'inner', axis=0, tiled=T...]
    another operation x2 -> x0, loops' own time: 27.7 us -> none  [the longest x1 22.3 us: carried_in(): return lax.fori_loop(0, count - 1, turn, so_far)]
    dynamic_slice x39 -> x0, local copies, waits for them, and re-layouts: 23.3 us -> none  [the longest x31 20.6 us: turn(): longer = join(so_far, jax.tree.map(lambda part: part[position], pieces))]
    convert_element_type x6 -> x0, other arithmetic: 10 us -> none  [the longest x4 5.24 us: span_step(): reach_mask = (segment == before).astype(jnp.float32)]
  transfers between devices with their start and end apart: 3 -> 0, of which waited for: 2 -> 0; matrix products, arithmetic and copies ran while one was open for 5% -> 0% of each run, Pallas kernels for 0% -> 0%
where the time goes in v1:
time: 117 us; the launch traced here: 116 us
  Pallas kernels  109 us (93%)
  local copies, waits for them, and re-layouts  7.41 us (6%)
    pallas_call x1, Pallas kernels, per_device(): pl.pallas_call(kernel, out_shape=jax.ShapeDtypeStruct((2048, 256), BF16),...  109 us
    unnamed x13, local copies, waits for them, and re-layouts  6.73 us

profile of v1, /device:TPU:1, one launch (start us, length us, event | category | flops | bytes accessed | tf_op | source)
XLA Modules:
  0.0 116.2 jit_solution(9978949133112154118)
XLA Ops:
  0.0 0.7 broadcast_in_dim.2.head_gain
  0.7 0.0 copy-start
  0.7 1.6 %copy-done = s32[256,2048]{1,0:T(8,128)S(1)} copy-done((s32[256,2048]{1,0:T(8,128)S(1)}, s32[256,2048]{1,0:T(8,128)}, u32[]{:S(2)}) %copy-start) | copy-done | bytes 2097176
  2.3 0.0 copy-start.1
  2.3 1.2 %copy-done.1 = bf16[256,2048]{1,0:T(8,128)(2,1)S(1)} copy-done((bf16[256,2048]{1,0:T(8,128)(2,1)S(1)}, bf16[256,2048]{1,0:T(8,128)(2,1)}, u32[]{:S(2)}) %copy-start.1) | copy-done | bytes 1048600
  3.5 0.0 copy-start.2
  3.5 0.9 copy-done.2
  4.4 0.0 copy-start.3
  4.4 0.7 copy-done.3
  5.1 0.0 copy-start.4
  5.1 0.7 copy-done.4
  5.8 0.0 copy-start.5
  5.8 0.7 copy-done.5
  6.4 108.8 %shard_map.73 = bf16[2048,256]{1,0:T(8,128)(2,1)S(1)} custom-call(bf16[256,2048]{1,0:T(8,128)(2,1)S(1)} %copy-done.1, f32[1,2048]{1,0:T(1,128)S(1)} %bitcast.2, f32[1,2048]{1,0:T(1,128)S(1)} %bitcast.3, s32[256,2048]{1,0:T(8,128)S(1)} %copy-done, bf16[3,64,256]{2,1,0:T(8,128)(2,1)S(1)} %copy-done.2, f32[8,256]{1,0:T(8,128)S(1)} %broadcast_in_dim.2.head_gain, ...), custom_call_target="tpu_custom_call" | custom-call | tf_op jit(solution)/shard_map/pallas_call | solution.py:535
  115.3 1.0 copy.9
Async XLA Ops:
  0.7 1.6 %copy-start = (s32[256,2048]{1,0:T(8,128)S(1)}, s32[256,2048]{1,0:T(8,128)}, u32[]{:S(2)}) copy-start(s32[256,2048]{1,0:T(8,128)} %mask_hbm.1) | copy-start | bytes 6291460
  2.3 1.2 %copy-start.1 = (bf16[256,2048]{1,0:T(8,128)(2,1)S(1)}, bf16[256,2048]{1,0:T(8,128)(2,1)}, u32[]{:S(2)}) copy-start(bf16[256,2048]{1,0:T(8,128)(2,1)} %tok_hbm.1) | copy-start | bytes 3145732
  3.5 0.9 copy-start.2
  4.4 0.7 copy-start.3
  5.1 0.7 copy-start.4
  5.8 0.7 copy-start.5

commit v2 on v1

--- a/solution.py
+++ b/solution.py
@@ -12,7 +12,7 @@
 PARTS = 4
 PART = OWN // PARTS
 RANGES = ((1, 2), (0, 1))
-UNITS = ((0, 0), (1, 0), (0, 1), (1, 1))
+UNITS = ((1, 0), (0, 0), (1, 1), (0, 1))
 
 
 def slot_of(dist):
@@ -30,9 +30,9 @@
 
 
 def kernel(
-    tok_hbm, gain, bias, mask_hbm, proj_hbm, head_gain, traj, out,
-    tok, mask, x_all, w_all, qkv, inside, a_out, rz, local_c, t_all, tp, ps, p_all, c_out, cr, gains, outs,
-    in_sem, wz_send, wz_recv, ring_send, ring_recv, tok_send, tok_recv, fwd_send, sib_recv, hg_send, hg_recv,
+    tok_hbm, gain_hbm, bias_hbm, mask_hbm, proj_hbm, head_gain, traj_hbm, out,
+    gain, bias, traj, tok, mask, x_all, w_all, qkv, inside, a_out, rz, local_c, t_all, tp, ps, p_all, c_out, cr, gains, outs,
+    in_sem, small_sem, wz_send, wz_recv, ring_send, ring_recv, tok_send, tok_recv, fwd_send, sib_recv, hg_send, hg_recv,
     rz_send, rz_recv, a2a_send, a2a_recv, cr_send, cr_recv, out_send, out_recv,
 ):
     outer, z = lax.axis_index("outer"), lax.axis_index("inner")
@@ -73,7 +73,14 @@
             pltpu.make_async_copy(mask_hbm.at[rows], mask.at[rows], in_sem.at[1, i]),
         )
 
-    for i in range(PARTS):
+    small_copies = (
+        pltpu.make_async_copy(gain_hbm, gain, small_sem.at[0]),
+        pltpu.make_async_copy(bias_hbm, bias, small_sem.at[1]),
+        pltpu.make_async_copy(traj_hbm, traj, small_sem.at[2]),
+    )
+    for copy in in_copies(0) + small_copies:
+        copy.start()
+    for i in range(1, PARTS):
         for copy in in_copies(i):
             copy.start()
 
@@ -90,7 +97,6 @@
 
     lax.fori_loop(1, 16, greet_column, 0)
     lax.fori_loop(1, 16, greet_plane, 0)
-    pl.semaphore_wait(barrier, 30)
 
     def wz_copy(d, r):
         first, count = RANGES[r]
@@ -98,8 +104,8 @@
         dst = w_all.at[slot_of(d), pl.ds(first, count), cx, cy, pl.ds(core * 64, 64)]
         return src, dst, wz_send.at[d, r], wz_recv.at[slot_of(d), r, core], column_dev(core_of(d), plane_at(z, d))
 
-    for r in range(2):
-        for d in (3, 2, 1, 0):
+    def send_weights(r):
+        for d in (0, 1, 2, 3):
             src, dst, send, recv, device = wz_copy(d, r)
             if d == 0:
 
@@ -113,16 +119,18 @@
 
             else:
                 remote(src, dst, send, recv, device).start()
-    for d in range(4):
-
-        @pl.when((core == core_of(d)) if d else (core == 2))
+
+    def send_gains():
+        for d in range(4):
+
+            @pl.when((core == core_of(d)) if d else (core == 2))
+            def _():
+                s = slot_of(d)
+                remote(head_gain, gains.at[s], hg_send.at[s], hg_recv.at[s], column_dev(core, plane_at(z, d))).start()
+
+        @pl.when(core == 0)
         def _():
-            s = slot_of(d)
-            remote(head_gain, gains.at[s], hg_send.at[s], hg_recv.at[s], column_dev(core, plane_at(z, d))).start()
-
-    @pl.when(core == 0)
-    def _():
-        gains[1] = head_gain[...]
+            pltpu.make_async_copy(head_gain, gains.at[1], small_sem.at[3]).start()
 
     def wait_wz(u):
         s, r = UNITS[u]
@@ -158,6 +166,13 @@
         wait_wz(u)
         for way in range(2):
             ref = block(u, chip)
+            remote(ref, ref, *ring_sems(u, 0, way), a_devices[way]).start()
+
+    def a_direct(u):
+        wait_wz(u)
+        ref = block(u, chip)
+        remote(ref, ref, *ring_sems(u, 1, 0), plane_dev(chip_at((along + 2) % 4, across))).start()
+        for way in range(2):
             remote(ref, ref, *ring_sems(u, 0, way), a_devices[way]).start()
 
     def wait_ring(u, stage):
@@ -185,7 +200,11 @@
                 remote(ref, ref, *ring_sems(u, stage, way), b_devices[way]).start()
 
     def b1(u):
-        wait_ring(u, 1)
+        if u == 0:
+            wait_ring(u, 0)
+            wait_for(block(u, 0), ring_recv.at[u, 1, 0])
+        else:
+            wait_ring(u, 1)
         b_send(u, 2, (across, across), False)
 
     def b2(u):
@@ -197,6 +216,9 @@
 
     def ring_wait_sends(u):
         for stage in range(4):
+            if u == 0 and stage == 1:
+                wait_for(block(u, 0), ring_send.at[u, 1, 0])
+                continue
             for way in range(2):
                 half = 64 * way if stage in (1, 3) else None
                 ref = line_y(u, 0, half) if stage >= 2 else block(u, 0, half)
@@ -335,7 +357,7 @@
         for j in range(8):
             for s in range(2):
                 total = local_c[j, s] + p_all[s * 64:(s + 1) * 64, :] * reach
-                c_out[s, j // 4, j % 4] = total.astype(BF16)
+                c_out[s, j // 4, j % 4] = total
             reach = reach * keeps(chip_first + j * SPAN, SPAN)
         for s in range(2):
             mine = dists[s]
@@ -377,111 +399,119 @@
 
         lax.fori_loop(0, 2, one_span, 0)
 
-    def finish(s):
-        def one_span(c, carry):
-            first = span_first(c)
-            rows = first + lax.broadcasted_iota(I32, (SPAN, 1), 0)
+    def finish(s, c):
+        first = span_first(c)
+        for top in (0, 256):
+            rows = first + top + lax.broadcasted_iota(I32, (256, 1), 0)
             reached = start_of(rows) < first
             for h in range(2):
                 columns = slice(h * HEAD, (h + 1) * HEAD)
-                term = jnp.dot(qkv[s, 0, c, :, columns], cr[s, c, columns, :], preferred_element_type=F32)
-                mixed = inside[s, c, :, columns] + jnp.where(reached, term, 0.0)
+                queries = qkv[s, 0, c, top:top + 256, columns]
+                state = cr[s, c, columns, :]
+                high = state.astype(BF16)
+                low = (state - high.astype(F32)).astype(BF16)
+                term = jnp.dot(queries, high, preferred_element_type=F32)
+                term += jnp.dot(queries, low, preferred_element_type=F32)
+                mixed = inside[s, c, top:top + 256, columns] + jnp.where(reached, term, 0.0)
                 scale_back = lax.rsqrt(jnp.mean(mixed * mixed, axis=-1, keepdims=True) + 1e-06)
-                outs[s, c, :, columns] = (mixed * scale_back * gains[s, 0:1, columns]).astype(BF16)
-            return carry
-
-        lax.fori_loop(0, 2, one_span, 0)
-
-    def send_out(s):
+                outs[s, c, top:top + 256, columns] = (mixed * scale_back * gains[s, :, columns]).astype(BF16)
+
+    def send_out(s, c):
         rows = pl.ds(pl.multiple_of(pair * SPAN, SPAN), SPAN)
-        for c in range(2):
-            device = column_dev(c, planes[s])
-            args = (outs.at[s, c], out.at[rows])
-            if s == 1 and c == 0:
-
-                @pl.when(core == 0)
-                def _():
-                    pltpu.make_async_copy(*args, out_recv.at[pair]).start()
-
-                @pl.when(core == 1)
-                def _():
-                    remote(*args, out_send.at[s, c], out_recv.at[pair], device).start()
-
-            else:
+        device = column_dev(c, planes[s])
+        args = (outs.at[s, c], out.at[rows])
+        if s == 1 and c == 0:
+
+            @pl.when(core == 0)
+            def _():
+                pltpu.make_async_copy(*args, out_recv.at[pair]).start()
+
+            @pl.when(core == 1)
+            def _():
                 remote(*args, out_send.at[s, c], out_recv.at[pair], device).start()
 
+        else:
+            remote(*args, out_send.at[s, c], out_recv.at[pair], device).start()
+
+    for copy in small_copies:
+        copy.wait()
     normalize(0)
+    pl.semaphore_wait(barrier, 30)
     send_tokens(0)
-    a1(0)
+    send_weights(0)
     normalize(1)
     send_tokens(1)
-    a1(1)
+    a_direct(0)
     normalize(2)
     send_tokens(2)
-    a2(0)
     normalize(3)
     send_tokens(3)
+    send_weights(1)
+    send_gains()
     b1(0)
+    a1(1)
+    forward_tokens(0)
     a2(1)
+    b2(0)
     b1(1)
+    forward_tokens(1)
     a1(2)
     a1(3)
-    forward_tokens(0)
-    forward_tokens(1)
-    b2(0)
-    a2(2)
-    a2(3)
     b_done(0)
     for i in range(PARTS):
         wait_for(token_rows(1 - core, member, i), sib_recv.at[0, i])
     for w in (1, 2):
-        project(0, w, member)
+        project(1, w, member)
     forward_tokens(2)
+    a2(2)
+    a2(3)
     b2(1)
+    forward_tokens(3)
     b1(2)
-    forward_tokens(3)
     b1(3)
+    for i in range(PARTS):
+        wait_for(token_rows(1 - core, 1 - member, i), sib_recv.at[1, i])
+    for w in (1, 2):
+        project(1, w, 1 - member)
+    states(1)
+    send_states(1)
     b_done(1)
     for w in (1, 2):
-        project(1, w, member)
-    for i in range(PARTS):
-        wait_for(token_rows(1 - core, 1 - member, i), sib_recv.at[1, i])
-    for s in range(2):
-        for w in (1, 2):
-            project(s, w, 1 - member)
-        states(s)
-        send_states(s)
+        project(0, w, member)
+        project(0, w, 1 - member)
+    states(0)
+    send_states(0)
     b2(2)
+    wait_states(1)
+    wait_states(0)
+    chip_totals()
+    b2(3)
     b_done(2)
-    for s in range(2):
-        wait_states(s)
-    chip_totals()
+    for m in range(2):
+        project(1, 0, m)
+    prefixes()
+    b_done(3)
     for m in range(2):
         project(0, 0, m)
-    b2(3)
-    prefixes()
+    carried()
     inside_terms(0)
-    carried()
-    b_done(3)
-    for m in range(2):
-        project(1, 0, m)
     inside_terms(1)
-    wait_carried(0)
 
     @pl.when(core == 0)
     def _():
         wait_for(gains.at[0], hg_recv.at[0])
+        wait_for(gains.at[1], small_sem.at[3])
 
     @pl.when(core == 1)
     def _():
         for s in range(2):
             wait_for(gains.at[s], hg_recv.at[s])
 
-    finish(0)
-    send_out(0)
-    wait_carried(1)
-    finish(1)
-    send_out(1)
+    for s in range(2):
+        wait_carried(s)
+        for c in range(2):
+            finish(s, c)
+            send_out(s, c)
 
     for r in range(2):
         first, count = RANGES[r]
@@ -511,7 +541,7 @@
     for s in range(2):
         for i in range(3):
             wait_for(rz.at[s, :, 0], rz_send.at[s, i])
-            wait_for(rz.at[s, :, 0], cr_send.at[s, i])
+            wait_for(c_out.at[s, :, 0], cr_send.at[s, i])
     for i in range(2):
         wait_for(tp.at[pl.ds(0, 15)], a2a_send.at[i])
     for s in range(2):
@@ -535,9 +565,12 @@
     return pl.pallas_call(
         kernel,
         out_shape=jax.ShapeDtypeStruct((2048, 256), BF16),
-        in_specs=[any_spec, vmem, vmem, any_spec, any_spec, vmem, pl.BlockSpec(memory_space=pltpu.SMEM)],
+        in_specs=[any_spec] * 7,
         out_specs=vmem,
         scratch_shapes=[
+            pltpu.VMEM((1, D), F32),
+            pltpu.VMEM((1, D), F32),
+            pltpu.SMEM((8,), I32),
             pltpu.VMEM((OWN, D), BF16),
             pltpu.VMEM((OWN, D), I32),
             pltpu.VMEM((2, 2, OWN, D), BF16),
@@ -551,11 +584,12 @@
             pltpu.VMEM((16, 8, HEAD), F32),
             pltpu.VMEM((16, 8, HEAD), F32),
             pltpu.VMEM((128, HEAD), F32),
-            pltpu.VMEM((2, 2, 4, 64, HEAD), BF16),
-            pltpu.VMEM((2, 2, 256, HEAD), BF16),
-            pltpu.VMEM((2, 8, 256), F32),
+            pltpu.VMEM((2, 2, 4, 64, HEAD), F32),
+            pltpu.VMEM((2, 2, 256, HEAD), F32),
+            pltpu.VMEM((2, 1, 256), F32),
             pltpu.VMEM((2, 2, SPAN, 256), BF16),
             dma((2, PARTS)),
+            dma((4,)),
             dma((4, 2)),
             dma((2, 2, 2)),
             dma((4, 4, 2)),
@@ -576,11 +610,11 @@
             dma((4,)),
         ],
         compiler_params=pltpu.CompilerParams(
-            collective_id=0, has_side_effects=True, vmem_limit_bytes=48 * 1024 * 1024
+            collective_id=0, has_side_effects=True, vmem_limit_bytes=63 * 1024 * 1024
         ),
     )(
         tokens, norm_gain.reshape(1, D), norm_bias.reshape(1, D), keep_mask, projection,
-        jnp.broadcast_to(head_gain[None, :], (8, 256)), traj_starts,
+        head_gain.reshape(1, 256), traj_starts,
     )
 
 

time: 117 us -> 108 us (0.923)
  local copies, waits for them, and re-layouts: 7.41 us -> 2.26 us
  Pallas kernels: 109 us -> 105 us
    unnamed x13 -> x1, local copies, waits for them, and re-layouts: 6.73 us -> 2.26 us
    pallas_call x1, Pallas kernels: 109 us -> 105 us  [per_device(): pl.pallas_call(kernel, out_shape=jax.ShapeDtypeStruct((2048, 256), BF16),...]
where the time goes in v2:
time: 108 us; the launch traced here: 107 us
  Pallas kernels  105 us (97%)
  local copies, waits for them, and re-layouts  2.26 us (2%)
    pallas_call x1, Pallas kernels, per_device(): pl.pallas_call(kernel, out_shape=jax.ShapeDtypeStruct((2048, 256), BF16),...  105 us
    unnamed x1, local copies, waits for them, and re-layouts  2.26 us

profile of v2, /device:TPU:1, one launch (start us, length us, event | category | flops | bytes accessed | tf_op | source)
XLA Modules:
  0.0 107.5 jit_solution(10575213729650784052)
XLA Ops:
  0.0 105.2 %shard_map.73 = bf16[2048,256]{1,0:T(8,128)(2,1)} custom-call(bf16[256,2048]{1,0:T(8,128)(2,1)} %tok_hbm.1, f32[1,2048]{1,0:T(1,128)} %bitcast.3, f32[1,2048]{1,0:T(1,128)} %bitcast.4, s32[256,2048]{1,0:T(8,128)} %mask_hbm.1, bf16[3,64,256]{2,1,0:T(8,128)(2,1)} %proj_hbm.1, f32[1,256]{1,0:T(1,128)} %bitcast.5, s32[8]{0:T(128)} %traj_hbm.1), custom_call_target="tpu_custom_call" | custom-call | tf_op jit(solution)/shard_map/pallas_call | solution.py:565
  105.2 2.3 %copy.9 = bf16[2048,256]{1,0:T(8,128)(2,1)} copy(bf16[2048,256]{1,0:T(8,128)(2,1)} %shard_map.73) | data formatting | bytes 2097152

commit v3 on v2

--- a/solution.py
+++ b/solution.py
@@ -9,10 +9,11 @@
 F32, BF16, I32 = jnp.float32, jnp.bfloat16, jnp.int32
 D, HEAD, SPAN = 2048, 128, 512
 OWN = 256
+DIRECT = 2
 PARTS = 4
 PART = OWN // PARTS
-RANGES = ((1, 2), (0, 1))
-UNITS = ((1, 0), (0, 0), (1, 1), (0, 1))
+QUERY, KEY, VALUE = 0, 1, 2
+UNITS = ((1, KEY), (1, VALUE), (0, KEY), (0, VALUE), (1, QUERY), (0, QUERY))
 
 
 def slot_of(dist):
@@ -31,9 +32,9 @@
 
 def kernel(
     tok_hbm, gain_hbm, bias_hbm, mask_hbm, proj_hbm, head_gain, traj_hbm, out,
-    gain, bias, traj, tok, mask, x_all, w_all, qkv, inside, a_out, rz, local_c, t_all, tp, ps, p_all, c_out, cr, gains, outs,
+    gain, bias, traj, tok, mask, x_all, w_all, qkv, inside, a_out, rz, local_c, t_all, tp, ps, local_in, prefix_in, gains, outs,
     in_sem, small_sem, wz_send, wz_recv, ring_send, ring_recv, tok_send, tok_recv, fwd_send, sib_recv, hg_send, hg_recv,
-    rz_send, rz_recv, a2a_send, a2a_recv, cr_send, cr_recv, out_send, out_recv,
+    rz_send, rz_recv, a2a_send, a2a_recv, local_send, local_recv, prefix_send, prefix_recv, out_send, out_recv,
 ):
     outer, z = lax.axis_index("outer"), lax.axis_index("inner")
     core, chip = outer % 2, outer // 2
@@ -65,6 +66,8 @@
 
     def wait_for(ref, sem):
         pltpu.make_async_copy(ref, ref, sem).wait()
+
+    sixty_three = prefix_in.at[pl.ds(0, 63)]
 
     def in_copies(i):
         rows = pl.ds(i * PART, PART)
@@ -98,15 +101,14 @@
     lax.fori_loop(1, 16, greet_column, 0)
     lax.fori_loop(1, 16, greet_plane, 0)
 
-    def wz_copy(d, r):
-        first, count = RANGES[r]
-        src = proj_hbm.at[pl.ds(first, count)]
-        dst = w_all.at[slot_of(d), pl.ds(first, count), cx, cy, pl.ds(core * 64, 64)]
-        return src, dst, wz_send.at[d, r], wz_recv.at[slot_of(d), r, core], column_dev(core_of(d), plane_at(z, d))
-
-    def send_weights(r):
-        for d in (0, 1, 2, 3):
-            src, dst, send, recv, device = wz_copy(d, r)
+    def wz_copy(d, w):
+        src = proj_hbm.at[w]
+        dst = w_all.at[slot_of(d), w, cx, cy, pl.ds(core * 64, 64)]
+        return src, dst, wz_send.at[d, w], wz_recv.at[slot_of(d), w, core], column_dev(core_of(d), plane_at(z, d))
+
+    def send_weights(w, which):
+        for d in which:
+            src, dst, send, recv, device = wz_copy(d, w)
             if d == 0:
 
                 @pl.when(core == 0)
@@ -133,28 +135,21 @@
             pltpu.make_async_copy(head_gain, gains.at[1], small_sem.at[3]).start()
 
     def wait_wz(u):
-        s, r = UNITS[u]
-        first, count = RANGES[r]
+        s, w = UNITS[u]
         for half in range(2):
-            wait_for(w_all.at[s, pl.ds(first, count), 0, 0, pl.ds(half * 64, 64)], wz_recv.at[s, r, half])
+            wait_for(w_all.at[s, w, 0, 0, pl.ds(half * 64, 64)], wz_recv.at[s, w, half])
 
     def block(u, chip_id, rows=None):
-        s, r = UNITS[u]
-        first, count = RANGES[r]
-        ref = w_all.at[s, pl.ds(first, count), chip_id // 4, chip_id % 4]
+        ref = w_all.at[(*UNITS[u], chip_id // 4, chip_id % 4)]
+        return ref if rows is None else ref.at[pl.ds(rows, 64)]
+
+    def line_x(u, b, rows=None):
+        ref = w_all.at[(*UNITS[u], slice(None), b)]
         return ref if rows is None else ref.at[:, pl.ds(rows, 64)]
 
-    def line_x(u, b, rows=None):
-        s, r = UNITS[u]
-        first, count = RANGES[r]
-        ref = w_all.at[s, pl.ds(first, count), :, b]
-        return ref if rows is None else ref.at[:, :, pl.ds(rows, 64)]
-
     def line_y(u, b, rows=None):
-        s, r = UNITS[u]
-        first, count = RANGES[r]
-        ref = w_all.at[s, pl.ds(first, count), b]
-        return ref if rows is None else ref.at[:, :, pl.ds(rows, 64)]
+        ref = w_all.at[(*UNITS[u], b)]
+        return ref if rows is None else ref.at[:, pl.ds(rows, 64)]
 
     def ring_sems(u, stage, way):
         return ring_send.at[u, stage, way], ring_recv.at[u, stage, way]
@@ -200,7 +195,7 @@
                 remote(ref, ref, *ring_sems(u, stage, way), b_devices[way]).start()
 
     def b1(u):
-        if u == 0:
+        if u < DIRECT:
             wait_ring(u, 0)
             wait_for(block(u, 0), ring_recv.at[u, 1, 0])
         else:
@@ -216,7 +211,7 @@
 
     def ring_wait_sends(u):
         for stage in range(4):
-            if u == 0 and stage == 1:
+            if u < DIRECT and stage == 1:
                 wait_for(block(u, 0), ring_send.at[u, 1, 0])
                 continue
             for way in range(2):
@@ -317,48 +312,21 @@
         for s in range(2):
             total = jnp.zeros((64, HEAD), F32)
             for j in range(8):
-                local_c[j, s] = total
+                local_c[s, j // 4, j % 4] = total
                 total = total * keeps(chip_first + j * SPAN, SPAN) + rz[s, j // 4, j % 4].astype(F32)
             t_all[s * 64:(s + 1) * 64, :] = total
 
         def send(i, carry):
             other = (chip + i) % 16
             remote(
-                t_all.at[pl.ds(pl.multiple_of(other * 8, 8), 8)], tp.at[chip], a2a_send.at[0], a2a_recv.at[0],
-                plane_dev(other),
+                t_all.at[pl.ds(pl.multiple_of(other * 8, 8), 8)], tp.at[chip], a2a_send, a2a_recv, plane_dev(other)
             ).start()
             return carry
 
         lax.fori_loop(1, 16, send, 0)
         tp[chip] = t_all[pl.ds(pl.multiple_of(chip * 8, 8), 8), :]
 
-    def prefixes():
-        wait_for(tp.at[pl.ds(0, 15)], a2a_recv.at[0])
-        total = jnp.zeros((8, HEAD), F32)
-        for k in range(16):
-            ps[k] = total
-            if k < 15:
-                total = total * keeps(k * 8 * SPAN, 8 * SPAN) + tp[k]
-
-        def send(i, carry):
-            other = (chip + i) % 16
-            remote(
-                ps.at[other], p_all.at[pl.ds(pl.multiple_of(chip * 8, 8), 8)], a2a_send.at[1], a2a_recv.at[1],
-                plane_dev(other),
-            ).start()
-            return carry
-
-        lax.fori_loop(1, 16, send, 0)
-        p_all[pl.ds(pl.multiple_of(chip * 8, 8), 8), :] = ps[chip]
-
-    def carried():
-        wait_for(tp.at[pl.ds(0, 15)], a2a_recv.at[1])
-        reach = jnp.ones((), F32)
-        for j in range(8):
-            for s in range(2):
-                total = local_c[j, s] + p_all[s * 64:(s + 1) * 64, :] * reach
-                c_out[s, j // 4, j % 4] = total
-            reach = reach * keeps(chip_first + j * SPAN, SPAN)
+    def send_local():
         for s in range(2):
             mine = dists[s]
             rows = pl.ds(pl.multiple_of(mine * 64, 64), 64)
@@ -366,16 +334,53 @@
                 other = (mine + i) % 4
                 plane = plane_at(planes[s], other)
                 remote(
-                    c_out.at[s, :, plane // 2], cr.at[slot_of(other), :, rows],
-                    cr_send.at[s, i - 1], cr_recv.at[slot_of(other), mine],
+                    local_c.at[s, :, plane // 2], local_in.at[slot_of(other), :, rows],
+                    local_send.at[s, i - 1], local_recv.at[slot_of(other), mine],
                     column_dev(core_of(other), plane),
                 ).start()
-            cr[s, :, rows, :] = c_out[s, :, pair]
-
-    def wait_carried(s):
+            local_in[s, :, rows, :] = local_c[s, :, pair]
+
+    def prefixes():
+        wait_for(tp.at[pl.ds(0, 15)], a2a_recv)
+        total = jnp.zeros((8, HEAD), F32)
+        for k in range(16):
+            ps[k] = total
+            if k < 15:
+                total = total * keeps(k * 8 * SPAN, 8 * SPAN) + tp[k]
+        slot = chip // 8
+        mine = jnp.where(slot == 0, dists[0], dists[1])
+        head_plane = jnp.where(slot == 0, planes[0], planes[1])
+        spot = mine * 8 + chip % 8
+
+        def to_chip(i, carry):
+            other = (chip + i) % 16
+            for near in range(4):
+                dist = (mine + near) % 4
+                plane = plane_at(head_plane, dist)
+                target = (other * 2 + core_of(dist), plane)
+                if near == 0:
+
+                    @pl.when(i != 0)
+                    def _():
+                        remote(
+                            ps.at[other], prefix_in.at[slot_of(dist) * 32 + spot], prefix_send, prefix_recv, target
+                        ).start()
+                else:
+                    remote(
+                        ps.at[other], prefix_in.at[slot_of(dist) * 32 + spot], prefix_send, prefix_recv, target
+                    ).start()
+            return carry
+
+        lax.fori_loop(0, 16, to_chip, 0)
+        prefix_in[slot * 32 + spot] = ps[chip]
+
+    def wait_prefix():
+        wait_for(sixty_three, prefix_recv)
+
+    def wait_local(s):
         for i in range(1, 4):
             spot = (dists[s] + i) % 4
-            wait_for(cr.at[s, :, pl.ds(0, 64)], cr_recv.at[s, spot])
+            wait_for(local_in.at[s, :, pl.ds(0, 64)], local_recv.at[s, spot])
 
     def inside_terms(s):
         def one_span(c, carry):
@@ -401,13 +406,18 @@
 
     def finish(s, c):
         first = span_first(c)
+        reach = jnp.ones((), F32)
+        for j in range(7):
+            going_on = reach * keeps(chip_first + j * SPAN, SPAN)
+            reach = jnp.where(j < c * 4 + pair, going_on, reach)
         for top in (0, 256):
             rows = first + top + lax.broadcasted_iota(I32, (256, 1), 0)
             reached = start_of(rows) < first
             for h in range(2):
                 columns = slice(h * HEAD, (h + 1) * HEAD)
                 queries = qkv[s, 0, c, top:top + 256, columns]
-                state = cr[s, c, columns, :]
+                prefix = prefix_in[s * 32 + h * 16:s * 32 + (h + 1) * 16].reshape(HEAD, HEAD)
+                state = local_in[s, c, columns, :] + prefix * reach
                 high = state.astype(BF16)
                 low = (state - high.astype(F32)).astype(BF16)
                 term = jnp.dot(queries, high, preferred_element_type=F32)
@@ -438,62 +448,75 @@
     normalize(0)
     pl.semaphore_wait(barrier, 30)
     send_tokens(0)
-    send_weights(0)
+    send_weights(KEY, (0, 1))
+    send_weights(VALUE, (0, 1))
+    send_weights(KEY, (3, 2))
+    send_weights(VALUE, (3, 2))
     normalize(1)
     send_tokens(1)
-    a_direct(0)
     normalize(2)
     send_tokens(2)
+    a_direct(0)
     normalize(3)
     send_tokens(3)
-    send_weights(1)
+    a_direct(1)
+    send_weights(QUERY, (0, 1, 2, 3))
     send_gains()
     b1(0)
-    a1(1)
+    a1(2)
+    b1(1)
+    a1(3)
     forward_tokens(0)
-    a2(1)
+    a2(2)
     b2(0)
-    b1(1)
+    a2(3)
+    b1(2)
     forward_tokens(1)
-    a1(2)
-    a1(3)
+    b2(1)
+    a1(4)
     b_done(0)
     for i in range(PARTS):
         wait_for(token_rows(1 - core, member, i), sib_recv.at[0, i])
-    for w in (1, 2):
-        project(1, w, member)
+    project(1, KEY, member)
+    b1(3)
+    a1(5)
+    b_done(1)
+    project(1, VALUE, member)
     forward_tokens(2)
-    a2(2)
-    a2(3)
-    b2(1)
+    b2(2)
+    a2(4)
+    b1(4)
+    b2(3)
+    a2(5)
+    b_done(2)
+    project(0, KEY, member)
     forward_tokens(3)
-    b1(2)
-    b1(3)
+    b1(5)
     for i in range(PARTS):
         wait_for(token_rows(1 - core, 1 - member, i), sib_recv.at[1, i])
-    for w in (1, 2):
-        project(1, w, 1 - member)
+    project(1, KEY, 1 - member)
+    project(1, VALUE, 1 - member)
     states(1)
     send_states(1)
-    b_done(1)
-    for w in (1, 2):
-        project(0, w, member)
-        project(0, w, 1 - member)
+    project(0, KEY, 1 - member)
+    b_done(3)
+    project(0, VALUE, member)
+    project(0, VALUE, 1 - member)
     states(0)
     send_states(0)
-    b2(2)
+    b2(4)
+    b2(5)
     wait_states(1)
     wait_states(0)
     chip_totals()
-    b2(3)
-    b_done(2)
+    send_local()
+    b_done(4)
     for m in range(2):
-        project(1, 0, m)
+        project(1, QUERY, m)
     prefixes()
-    b_done(3)
+    b_done(5)
     for m in range(2):
-        project(0, 0, m)
-    carried()
+        project(0, QUERY, m)
     inside_terms(0)
     inside_terms(1)
 
@@ -507,21 +530,23 @@
         for s in range(2):
             wait_for(gains.at[s], hg_recv.at[s])
 
+    wait_local(0)
+    wait_local(1)
+    wait_prefix()
     for s in range(2):
-        wait_carried(s)
         for c in range(2):
             finish(s, c)
             send_out(s, c)
 
-    for r in range(2):
-        first, count = RANGES[r]
-        ref = w_all.at[0, pl.ds(first, count), 0, 0, pl.ds(0, 64)]
+    ref = w_all.at[0, 0, 0, 0, pl.ds(0, 64)]
+    for w in range(3):
         for d in (1, 2, 3):
-            wait_for(ref, wz_send.at[d, r])
-
-        @pl.when(core == 1)
-        def _():
-            wait_for(ref, wz_send.at[0, r])
+            wait_for(ref, wz_send.at[d, w])
+
+    @pl.when(core == 1)
+    def _():
+        for w in range(3):
+            wait_for(ref, wz_send.at[0, w])
 
     @pl.when(core == 0)
     def _():
@@ -532,7 +557,7 @@
         for s in range(2):
             wait_for(gains.at[s], hg_send.at[s])
 
-    for u in range(4):
+    for u in range(len(UNITS)):
         ring_wait_sends(u)
     for i in range(PARTS):
         ref = token_rows(0, 0, i)
@@ -541,9 +566,9 @@
     for s in range(2):
         for i in range(3):
             wait_for(rz.at[s, :, 0], rz_send.at[s, i])
-            wait_for(c_out.at[s, :, 0], cr_send.at[s, i])
-    for i in range(2):
-        wait_for(tp.at[pl.ds(0, 15)], a2a_send.at[i])
+            wait_for(local_c.at[s, :, 0], local_send.at[s, i])
+    wait_for(tp.at[pl.ds(0, 15)], a2a_send)
+    wait_for(sixty_three, prefix_send)
     for s in range(2):
         for c in range(2):
             if s == 1 and c == 0:
@@ -560,13 +585,12 @@
 
 def per_device(tokens, norm_gain, norm_bias, keep_mask, projection, head_gain, traj_starts):
     any_spec = pl.BlockSpec(memory_space=pl.ANY)
-    vmem = pl.BlockSpec(memory_space=pltpu.VMEM)
     dma = pltpu.SemaphoreType.DMA
     return pl.pallas_call(
         kernel,
         out_shape=jax.ShapeDtypeStruct((2048, 256), BF16),
         in_specs=[any_spec] * 7,
-        out_specs=vmem,
+        out_specs=any_spec,
         scratch_shapes=[
             pltpu.VMEM((1, D), F32),
             pltpu.VMEM((1, D), F32),
@@ -579,21 +603,20 @@
             pltpu.VMEM((2, 2, SPAN, 256), F32),
             pltpu.VMEM((2, 2, 256, HEAD), BF16),
             pltpu.VMEM((2, 2, 4, 64, HEAD), BF16),
-            pltpu.VMEM((8, 2, 64, HEAD), F32),
+            pltpu.VMEM((2, 2, 4, 64, HEAD), F32),
             pltpu.VMEM((128, HEAD), F32),
             pltpu.VMEM((16, 8, HEAD), F32),
             pltpu.VMEM((16, 8, HEAD), F32),
-            pltpu.VMEM((128, HEAD), F32),
-            pltpu.VMEM((2, 2, 4, 64, HEAD), F32),
             pltpu.VMEM((2, 2, 256, HEAD), F32),
+            pltpu.VMEM((64, 8, HEAD), F32),
             pltpu.VMEM((2, 1, 256), F32),
             pltpu.VMEM((2, 2, SPAN, 256), BF16),
             dma((2, PARTS)),
             dma((4,)),
-            dma((4, 2)),
-            dma((2, 2, 2)),
-            dma((4, 4, 2)),
-            dma((4, 4, 2)),
+            dma((4, 3)),
+            dma((2, 3, 2)),
+            dma((len(UNITS), 4, 2)),
+            dma((len(UNITS), 4, 2)),
             dma((2, PARTS)),
             dma((PARTS,)),
             dma((PARTS,)),
@@ -602,10 +625,12 @@
             dma((2,)),
             dma((2, 3)),
             dma((2, 4)),
-            dma((2,)),
-            dma((2,)),
+            dma(()),
+            dma(()),
             dma((2, 3)),
             dma((2, 4)),
+            dma(()),
+            dma(()),
             dma((2, 2)),
             dma((4,)),
         ],

time: 108 us -> 109 us (level)
    pallas_call x1, Pallas kernels: 105 us -> 106 us  [per_device(): pl.pallas_call(kernel, out_shape=jax.ShapeDtypeStruct((2048, 256), BF16),...]
where the time goes in v3:
time: 109 us
  Pallas kernels  106 us (97%)
  local copies, waits for them, and re-layouts  2.26 us (2%)
    pallas_call x1, Pallas kernels, per_device(): pl.pallas_call(kernel, out_shape=jax.ShapeDtypeStruct((2048, 256), BF16),...  106 us
    unnamed x1, local copies, waits for them, and re-layouts  2.26 us

profile of v3, /device:TPU:1, one launch (start us, length us, event | category | flops | bytes accessed | tf_op | source)
XLA Modules:
  0.0 108.7 jit_solution(14284781379266802699)
XLA Ops:
  0.0 106.4 %shard_map.73 = bf16[2048,256]{1,0:T(8,128)(2,1)} custom-call(bf16[256,2048]{1,0:T(8,128)(2,1)} %tok_hbm.1, f32[1,2048]{1,0:T(1,128)} %bitcast.3, f32[1,2048]{1,0:T(1,128)} %bitcast.4, s32[256,2048]{1,0:T(8,128)} %mask_hbm.1, bf16[3,64,256]{2,1,0:T(8,128)(2,1)} %proj_hbm.1, f32[1,256]{1,0:T(1,128)} %bitcast.5, s32[8]{0:T(128)} %traj_hbm.1), custom_call_target="tpu_custom_call" | custom-call | tf_op jit(solution)/shard_map/pallas_call | solution.py:589
  106.4 2.3 %copy.9 = bf16[2048,256]{1,0:T(8,128)(2,1)} copy(bf16[2048,256]{1,0:T(8,128)(2,1)} %shard_map.73) | data formatting | bytes 2097152

commit v4 on v3

--- a/solution.py
+++ b/solution.py
@@ -9,11 +9,11 @@
 F32, BF16, I32 = jnp.float32, jnp.bfloat16, jnp.int32
 D, HEAD, SPAN = 2048, 128, 512
 OWN = 256
-DIRECT = 2
+DIRECT = 1
 PARTS = 4
 PART = OWN // PARTS
 QUERY, KEY, VALUE = 0, 1, 2
-UNITS = ((1, KEY), (1, VALUE), (0, KEY), (0, VALUE), (1, QUERY), (0, QUERY))
+UNITS = ((1, KEY), (0, KEY), (0, VALUE), (1, VALUE), (0, QUERY), (1, QUERY))
 
 
 def slot_of(dist):
@@ -67,8 +67,6 @@
     def wait_for(ref, sem):
         pltpu.make_async_copy(ref, ref, sem).wait()
 
-    sixty_three = prefix_in.at[pl.ds(0, 63)]
-
     def in_copies(i):
         rows = pl.ds(i * PART, PART)
         return (
@@ -271,6 +269,8 @@
         return jnp.where(start_of(first + (length - 1)) < first, 1.0, 0.0).astype(F32)
 
     chip_first = chip * 8 * SPAN
+
+    keep_spans = []
 
     def span_first(c):
         return chip_first + (c * 4 + pair) * SPAN
@@ -308,74 +308,69 @@
             spot = (pair + i) % 4
             wait_for(rz.at[s, :, spot], rz_recv.at[s, spot])
 
-    def chip_totals():
-        for s in range(2):
-            total = jnp.zeros((64, HEAD), F32)
-            for j in range(8):
-                local_c[s, j // 4, j % 4] = total
-                total = total * keeps(chip_first + j * SPAN, SPAN) + rz[s, j // 4, j % 4].astype(F32)
-            t_all[s * 64:(s + 1) * 64, :] = total
+    half = chip // 8
+    eighth = chip % 8
+
+    def chip_totals(s):
+        total = jnp.zeros((64, HEAD), F32)
+        for j in range(8):
+            local_c[s, j // 4, j % 4] = total.astype(BF16)
+            total = total * keep_spans[j] + rz[s, j // 4, j % 4].astype(F32)
+        t_all[s] = total
 
         def send(i, carry):
             other = (chip + i) % 16
             remote(
-                t_all.at[pl.ds(pl.multiple_of(other * 8, 8), 8)], tp.at[chip], a2a_send, a2a_recv, plane_dev(other)
+                t_all.at[s, pl.ds(pl.multiple_of((other % 8) * 8, 8), 8)], tp.at[s, chip], a2a_send.at[s], a2a_recv.at[s],
+                plane_dev(other),
             ).start()
             return carry
 
         lax.fori_loop(1, 16, send, 0)
-        tp[chip] = t_all[pl.ds(pl.multiple_of(chip * 8, 8), 8), :]
-
-    def send_local():
-        for s in range(2):
-            mine = dists[s]
-            rows = pl.ds(pl.multiple_of(mine * 64, 64), 64)
-            for i in range(1, 4):
-                other = (mine + i) % 4
-                plane = plane_at(planes[s], other)
-                remote(
-                    local_c.at[s, :, plane // 2], local_in.at[slot_of(other), :, rows],
-                    local_send.at[s, i - 1], local_recv.at[slot_of(other), mine],
-                    column_dev(core_of(other), plane),
-                ).start()
-            local_in[s, :, rows, :] = local_c[s, :, pair]
-
-    def prefixes():
-        wait_for(tp.at[pl.ds(0, 15)], a2a_recv)
+        tp[s, chip] = t_all[s, pl.ds(pl.multiple_of(eighth * 8, 8), 8), :]
+
+    def send_local(s):
+        mine = dists[s]
+        rows = pl.ds(pl.multiple_of(mine * 64, 64), 64)
+        for i in range(1, 4):
+            other = (mine + i) % 4
+            plane = plane_at(planes[s], other)
+            remote(
+                local_c.at[s, :, plane // 2], local_in.at[slot_of(other), :, rows],
+                local_send.at[s, i - 1], local_recv.at[slot_of(other), mine],
+                column_dev(core_of(other), plane),
+            ).start()
+        local_in[s, :, rows, :] = local_c[s, :, pair]
+
+    def prefixes(s):
+        wait_for(tp.at[s, pl.ds(0, 15)], a2a_recv.at[s])
         total = jnp.zeros((8, HEAD), F32)
         for k in range(16):
-            ps[k] = total
+            ps[s, k] = total
             if k < 15:
-                total = total * keeps(k * 8 * SPAN, 8 * SPAN) + tp[k]
-        slot = chip // 8
-        mine = jnp.where(slot == 0, dists[0], dists[1])
-        head_plane = jnp.where(slot == 0, planes[0], planes[1])
-        spot = mine * 8 + chip % 8
+                total = total * keeps(k * 8 * SPAN, 8 * SPAN) + tp[s, k]
+        mine = dists[s]
+        spot = mine * 8 + eighth
+        targets = []
+        for near in range(4):
+            dist = (mine + near) % 4
+            targets.append((core_of(dist), plane_at(planes[s], dist), prefix_in.at[slot_of(dist), spot], slot_of(dist)))
 
         def to_chip(i, carry):
-            other = (chip + i) % 16
-            for near in range(4):
-                dist = (mine + near) % 4
-                plane = plane_at(head_plane, dist)
-                target = (other * 2 + core_of(dist), plane)
+            other = half * 8 + (eighth + i) % 8
+            for near, (core_id, plane, dst, slot) in enumerate(targets):
+                copy = remote(ps.at[s, other], dst, prefix_send.at[s], prefix_recv.at[slot], (other * 2 + core_id, plane))
                 if near == 0:
-
-                    @pl.when(i != 0)
-                    def _():
-                        remote(
-                            ps.at[other], prefix_in.at[slot_of(dist) * 32 + spot], prefix_send, prefix_recv, target
-                        ).start()
+                    pl.when(i != 0)(copy.start)
                 else:
-                    remote(
-                        ps.at[other], prefix_in.at[slot_of(dist) * 32 + spot], prefix_send, prefix_recv, target
-                    ).start()
+                    copy.start()
             return carry
 
-        lax.fori_loop(0, 16, to_chip, 0)
-        prefix_in[slot * 32 + spot] = ps[chip]
-
-    def wait_prefix():
-        wait_for(sixty_three, prefix_recv)
+        lax.fori_loop(0, 8, to_chip, 0)
+        prefix_in[s, spot] = ps[s, chip]
+
+    def wait_prefix(s):
+        wait_for(prefix_in.at[s, pl.ds(0, 31)], prefix_recv.at[s])
 
     def wait_local(s):
         for i in range(1, 4):
@@ -408,16 +403,15 @@
         first = span_first(c)
         reach = jnp.ones((), F32)
         for j in range(7):
-            going_on = reach * keeps(chip_first + j * SPAN, SPAN)
-            reach = jnp.where(j < c * 4 + pair, going_on, reach)
+            reach = jnp.where(j < c * 4 + pair, reach * keep_spans[j], reach)
         for top in (0, 256):
             rows = first + top + lax.broadcasted_iota(I32, (256, 1), 0)
             reached = start_of(rows) < first
             for h in range(2):
                 columns = slice(h * HEAD, (h + 1) * HEAD)
                 queries = qkv[s, 0, c, top:top + 256, columns]
-                prefix = prefix_in[s * 32 + h * 16:s * 32 + (h + 1) * 16].reshape(HEAD, HEAD)
-                state = local_in[s, c, columns, :] + prefix * reach
+                prefix = prefix_in[s, h * 16:(h + 1) * 16].reshape(HEAD, HEAD)
+                state = local_in[s, c, columns, :].astype(F32) + prefix * reach
                 high = state.astype(BF16)
                 low = (state - high.astype(F32)).astype(BF16)
                 term = jnp.dot(queries, high, preferred_element_type=F32)
@@ -449,9 +443,9 @@
     pl.semaphore_wait(barrier, 30)
     send_tokens(0)
     send_weights(KEY, (0, 1))
-    send_weights(VALUE, (0, 1))
     send_weights(KEY, (3, 2))
     send_weights(VALUE, (3, 2))
+    send_weights(VALUE, (0, 1))
     normalize(1)
     send_tokens(1)
     normalize(2)
@@ -459,66 +453,67 @@
     a_direct(0)
     normalize(3)
     send_tokens(3)
-    a_direct(1)
-    send_weights(QUERY, (0, 1, 2, 3))
-    send_gains()
+    a1(1)
     b1(0)
     a1(2)
+    send_weights(QUERY, (3, 2, 1, 0))
+    send_gains()
+    forward_tokens(0)
+    keep_spans.extend(keeps(chip_first + j * SPAN, SPAN) for j in range(8))
+    a2(1)
+    a2(2)
+    a1(3)
+    b2(0)
     b1(1)
-    a1(3)
-    forward_tokens(0)
-    a2(2)
-    b2(0)
+    forward_tokens(1)
+    b1(2)
     a2(3)
-    b1(2)
-    forward_tokens(1)
-    b2(1)
-    a1(4)
-    b_done(0)
     for i in range(PARTS):
         wait_for(token_rows(1 - core, member, i), sib_recv.at[0, i])
+    b_done(0)
     project(1, KEY, member)
+    b2(1)
+    forward_tokens(2)
     b1(3)
-    a1(5)
+    b2(2)
     b_done(1)
-    project(1, VALUE, member)
-    forward_tokens(2)
-    b2(2)
-    a2(4)
-    b1(4)
-    b2(3)
-    a2(5)
-    b_done(2)
     project(0, KEY, member)
     forward_tokens(3)
-    b1(5)
+    b_done(2)
+    b2(3)
+    a1(4)
+    a1(5)
+    project(0, VALUE, member)
     for i in range(PARTS):
         wait_for(token_rows(1 - core, 1 - member, i), sib_recv.at[1, i])
+    project(0, KEY, 1 - member)
+    project(0, VALUE, 1 - member)
+    states(0)
+    send_states(0)
+    a2(4)
+    a2(5)
     project(1, KEY, 1 - member)
+    b1(4)
+    b1(5)
+    b_done(3)
+    project(1, VALUE, member)
     project(1, VALUE, 1 - member)
     states(1)
     send_states(1)
-    project(0, KEY, 1 - member)
-    b_done(3)
-    project(0, VALUE, member)
-    project(0, VALUE, 1 - member)
-    states(0)
-    send_states(0)
+    wait_states(0)
+    chip_totals(0)
+    send_local(0)
     b2(4)
+    prefixes(0)
+    wait_states(1)
+    chip_totals(1)
+    send_local(1)
     b2(5)
-    wait_states(1)
-    wait_states(0)
-    chip_totals()
-    send_local()
     b_done(4)
-    for m in range(2):
-        project(1, QUERY, m)
-    prefixes()
-    b_done(5)
     for m in range(2):
         project(0, QUERY, m)
     inside_terms(0)
-    inside_terms(1)
+    prefixes(1)
 
     @pl.when(core == 0)
     def _():
@@ -531,12 +526,19 @@
             wait_for(gains.at[s], hg_recv.at[s])
 
     wait_local(0)
+    wait_prefix(0)
+    for c in range(2):
+        finish(0, c)
+        send_out(0, c)
+    b_done(5)
+    for m in range(2):
+        project(1, QUERY, m)
+    inside_terms(1)
     wait_local(1)
-    wait_prefix()
-    for s in range(2):
-        for c in range(2):
-            finish(s, c)
-            send_out(s, c)
+    wait_prefix(1)
+    for c in range(2):
+        finish(1, c)
+        send_out(1, c)
 
     ref = w_all.at[0, 0, 0, 0, pl.ds(0, 64)]
     for w in range(3):
@@ -567,8 +569,9 @@
         for i in range(3):
             wait_for(rz.at[s, :, 0], rz_send.at[s, i])
             wait_for(local_c.at[s, :, 0], local_send.at[s, i])
-    wait_for(tp.at[pl.ds(0, 15)], a2a_send)
-    wait_for(sixty_three, prefix_send)
+    for s in range(2):
+        wait_for(tp.at[s, pl.ds(0, 15)], a2a_send.at[s])
+        wait_for(prefix_in.at[s, pl.ds(0, 31)], prefix_send.at[s])
     for s in range(2):
         for c in range(2):
             if s == 1 and c == 0:
@@ -603,12 +606,12 @@
             pltpu.VMEM((2, 2, SPAN, 256), F32),
             pltpu.VMEM((2, 2, 256, HEAD), BF16),
             pltpu.VMEM((2, 2, 4, 64, HEAD), BF16),
-            pltpu.VMEM((2, 2, 4, 64, HEAD), F32),
-            pltpu.VMEM((128, HEAD), F32),
-            pltpu.VMEM((16, 8, HEAD), F32),
-            pltpu.VMEM((16, 8, HEAD), F32),
-            pltpu.VMEM((2, 2, 256, HEAD), F32),
-            pltpu.VMEM((64, 8, HEAD), F32),
+            pltpu.VMEM((2, 2, 4, 64, HEAD), BF16),
+            pltpu.VMEM((2, 64, HEAD), F32),
+            pltpu.VMEM((2, 16, 8, HEAD), F32),
+            pltpu.VMEM((2, 16, 8, HEAD), F32),
+            pltpu.VMEM((2, 2, 256, HEAD), BF16),
+            pltpu.VMEM((2, 32, 8, HEAD), F32),
             pltpu.VMEM((2, 1, 256), F32),
             pltpu.VMEM((2, 2, SPAN, 256), BF16),
             dma((2, PARTS)),
@@ -625,12 +628,12 @@
             dma((2,)),
             dma((2, 3)),
             dma((2, 4)),
-            dma(()),
-            dma(()),
+            dma((2,)),
+            dma((2,)),
             dma((2, 3)),
             dma((2, 4)),
-            dma(()),
-            dma(()),
+            dma((2,)),
+            dma((2,)),
             dma((2, 2)),
             dma((4,)),
         ],

time: 109 us -> 104 us (0.954)
  Pallas kernels: 106 us -> 102 us
    pallas_call x1, Pallas kernels: 106 us -> 102 us  [per_device(): pl.pallas_call(kernel, out_shape=jax.ShapeDtypeStruct((2048, 256), BF16),...]
where the time goes in v4:
time: 104 us
  Pallas kernels  102 us (98%)
  local copies, waits for them, and re-layouts  2.26 us (2%)
    pallas_call x1, Pallas kernels, per_device(): pl.pallas_call(kernel, out_shape=jax.ShapeDtypeStruct((2048, 256), BF16),...  102 us
    unnamed x1, local copies, waits for them, and re-layouts  2.26 us

profile of v4, /device:TPU:1, one launch (start us, length us, event | category | flops | bytes accessed | tf_op | source)
XLA Modules:
  0.0 103.8 jit_solution(12274203560629637366)
XLA Ops:
  0.0 101.5 %shard_map.73 = bf16[2048,256]{1,0:T(8,128)(2,1)} custom-call(bf16[256,2048]{1,0:T(8,128)(2,1)} %tok_hbm.1, f32[1,2048]{1,0:T(1,128)} %bitcast.3, f32[1,2048]{1,0:T(1,128)} %bitcast.4, s32[256,2048]{1,0:T(8,128)} %mask_hbm.1, bf16[3,64,256]{2,1,0:T(8,128)(2,1)} %proj_hbm.1, f32[1,256]{1,0:T(1,128)} %bitcast.5, s32[8]{0:T(128)} %traj_hbm.1), custom_call_target="tpu_custom_call" | custom-call | tf_op jit(solution)/shard_map/pallas_call | solution.py:592
  101.5 2.3 %copy.9 = bf16[2048,256]{1,0:T(8,128)(2,1)} copy(bf16[2048,256]{1,0:T(8,128)(2,1)} %shard_map.73) | data formatting | bytes 2097152

commit v5 on v4

--- a/solution.py
+++ b/solution.py
@@ -14,10 +14,6 @@
 PART = OWN // PARTS
 QUERY, KEY, VALUE = 0, 1, 2
 UNITS = ((1, KEY), (0, KEY), (0, VALUE), (1, VALUE), (0, QUERY), (1, QUERY))
-
-
-def slot_of(dist):
-    return 1 - dist // 2
 
 
 def core_of(dist):
@@ -55,7 +51,8 @@
     def column_dev(core_id, plane):
         return (chip * 2 + core_id, plane)
 
-    dists = (3 - core, core)
+    dists = tuple(jnp.where((z + s) % 2 == 0, 2 * core, 3 - 2 * core) for s in range(2))
+    own_slot = z % 2
     step = 2 * member - 1
     planes = tuple((z + step * d + 8) % 8 for d in dists)
 
@@ -101,8 +98,8 @@
 
     def wz_copy(d, w):
         src = proj_hbm.at[w]
-        dst = w_all.at[slot_of(d), w, cx, cy, pl.ds(core * 64, 64)]
-        return src, dst, wz_send.at[d, w], wz_recv.at[slot_of(d), w, core], column_dev(core_of(d), plane_at(z, d))
+        dst = w_all.at[own_slot, w, cx, cy, pl.ds(core * 64, 64)]
+        return src, dst, wz_send.at[d, w], wz_recv.at[own_slot, w, core], column_dev(core_of(d), plane_at(z, d))
 
     def send_weights(w, which):
         for d in which:
@@ -121,16 +118,17 @@
                 remote(src, dst, send, recv, device).start()
 
     def send_gains():
-        for d in range(4):
-
-            @pl.when((core == core_of(d)) if d else (core == 2))
+        for d in (1, 2, 3):
+
+            @pl.when(core == core_of(d))
             def _():
-                s = slot_of(d)
-                remote(head_gain, gains.at[s], hg_send.at[s], hg_recv.at[s], column_dev(core, plane_at(z, d))).start()
+                remote(
+                    head_gain, gains.at[own_slot], hg_send.at[d - 1], hg_recv.at[own_slot], column_dev(core, plane_at(z, d))
+                ).start()
 
         @pl.when(core == 0)
         def _():
-            pltpu.make_async_copy(head_gain, gains.at[1], small_sem.at[3]).start()
+            pltpu.make_async_copy(head_gain, gains.at[own_slot], small_sem.at[3]).start()
 
     def wait_wz(u):
         s, w = UNITS[u]
@@ -297,8 +295,8 @@
         for i in range(1, 4):
             other = (mine + i) % 4
             remote(
-                a_out.at[s, :, pl.ds(pl.multiple_of(other * 64, 64), 64)], rz.at[slot_of(other), :, pair],
-                rz_send.at[s, i - 1], rz_recv.at[slot_of(other), pair],
+                a_out.at[s, :, pl.ds(pl.multiple_of(other * 64, 64), 64)], rz.at[s, :, pair],
+                rz_send.at[s, i - 1], rz_recv.at[s, pair],
                 column_dev(core_of(other), plane_at(planes[s], other)),
             ).start()
         rz[s, :, pair] = a_out[s, :, pl.ds(pl.multiple_of(mine * 64, 64), 64), :]
@@ -336,8 +334,8 @@
             other = (mine + i) % 4
             plane = plane_at(planes[s], other)
             remote(
-                local_c.at[s, :, plane // 2], local_in.at[slot_of(other), :, rows],
-                local_send.at[s, i - 1], local_recv.at[slot_of(other), mine],
+                local_c.at[s, :, plane // 2], local_in.at[s, :, rows],
+                local_send.at[s, i - 1], local_recv.at[s, mine],
                 column_dev(core_of(other), plane),
             ).start()
         local_in[s, :, rows, :] = local_c[s, :, pair]
@@ -354,12 +352,12 @@
         targets = []
         for near in range(4):
             dist = (mine + near) % 4
-            targets.append((core_of(dist), plane_at(planes[s], dist), prefix_in.at[slot_of(dist), spot], slot_of(dist)))
+            targets.append((core_of(dist), plane_at(planes[s], dist), prefix_in.at[s, spot]))
 
         def to_chip(i, carry):
             other = half * 8 + (eighth + i) % 8
-            for near, (core_id, plane, dst, slot) in enumerate(targets):
-                copy = remote(ps.at[s, other], dst, prefix_send.at[s], prefix_recv.at[slot], (other * 2 + core_id, plane))
+            for near, (core_id, plane, dst) in enumerate(targets):
+                copy = remote(ps.at[s, other], dst, prefix_send.at[s], prefix_recv.at[s], (other * 2 + core_id, plane))
                 if near == 0:
                     pl.when(i != 0)(copy.start)
                 else:
@@ -424,13 +422,13 @@
         rows = pl.ds(pl.multiple_of(pair * SPAN, SPAN), SPAN)
         device = column_dev(c, planes[s])
         args = (outs.at[s, c], out.at[rows])
-        if s == 1 and c == 0:
-
-            @pl.when(core == 0)
+        if c == 0:
+
+            @pl.when(dists[s] == 0)
             def _():
                 pltpu.make_async_copy(*args, out_recv.at[pair]).start()
 
-            @pl.when(core == 1)
+            @pl.when(dists[s] != 0)
             def _():
                 remote(*args, out_send.at[s, c], out_recv.at[pair], device).start()
 
@@ -442,10 +440,8 @@
     normalize(0)
     pl.semaphore_wait(barrier, 30)
     send_tokens(0)
-    send_weights(KEY, (0, 1))
-    send_weights(KEY, (3, 2))
-    send_weights(VALUE, (3, 2))
-    send_weights(VALUE, (0, 1))
+    send_weights(KEY, (0, 1, 2, 3))
+    send_weights(VALUE, (0, 1, 2, 3))
     normalize(1)
     send_tokens(1)
     normalize(2)
@@ -517,8 +513,8 @@
 
     @pl.when(core == 0)
     def _():
-        wait_for(gains.at[0], hg_recv.at[0])
-        wait_for(gains.at[1], small_sem.at[3])
+        wait_for(gains.at[0], hg_recv.at[1 - own_slot])
+        wait_for(gains.at[0], small_sem.at[3])
 
     @pl.when(core == 1)
     def _():
@@ -552,12 +548,12 @@
 
     @pl.when(core == 0)
     def _():
-        wait_for(gains.at[0], hg_send.at[0])
+        wait_for(gains.at[0], hg_send.at[2])
 
     @pl.when(core == 1)
     def _():
-        for s in range(2):
-            wait_for(gains.at[s], hg_send.at[s])
+        for i in range(2):
+            wait_for(gains.at[0], hg_send.at[i])
 
     for u in range(len(UNITS)):
         ring_wait_sends(u)
@@ -574,9 +570,9 @@
         wait_for(prefix_in.at[s, pl.ds(0, 31)], prefix_send.at[s])
     for s in range(2):
         for c in range(2):
-            if s == 1 and c == 0:
-
-                @pl.when(core == 1)
+            if c == 0:
+
+                @pl.when(dists[s] != 0)
                 def _():
                     wait_for(outs.at[s, c], out_send.at[s, c])
 
@@ -624,7 +620,7 @@
             dma((PARTS,)),
             dma((PARTS,)),
             dma((2, PARTS)),
-            dma((2,)),
+            dma((3,)),
             dma((2,)),
             dma((2, 3)),
             dma((2, 4)),

time: 104 us -> 98 us (0.942)
  Pallas kernels: 102 us -> 95.2 us
    pallas_call x1, Pallas kernels: 102 us -> 95.2 us  [per_device(): pl.pallas_call(kernel, out_shape=jax.ShapeDtypeStruct((2048, 256), BF16),...]
where the time goes in v5:
time: 98 us; the launch traced here: 97.5 us
  Pallas kernels  95.2 us (97%)
  local copies, waits for them, and re-layouts  2.26 us (2%)
    pallas_call x1, Pallas kernels, per_device(): pl.pallas_call(kernel, out_shape=jax.ShapeDtypeStruct((2048, 256), BF16),...  95.2 us
    unnamed x1, local copies, waits for them, and re-layouts  2.26 us

profile of v5, /device:TPU:1, one launch (start us, length us, event | category | flops | bytes accessed | tf_op | source)
XLA Modules:
  0.0 97.5 jit_solution(2881926285572117170)
XLA Ops:
  0.0 95.2 %shard_map.73 = bf16[2048,256]{1,0:T(8,128)(2,1)} custom-call(bf16[256,2048]{1,0:T(8,128)(2,1)} %tok_hbm.1, f32[1,2048]{1,0:T(1,128)} %bitcast.3, f32[1,2048]{1,0:T(1,128)} %bitcast.4, s32[256,2048]{1,0:T(8,128)} %mask_hbm.1, bf16[3,64,256]{2,1,0:T(8,128)(2,1)} %proj_hbm.1, f32[1,256]{1,0:T(1,128)} %bitcast.5, s32[8]{0:T(128)} %traj_hbm.1), custom_call_target="tpu_custom_call" | custom-call | tf_op jit(solution)/shard_map/pallas_call | solution.py:588
  95.2 2.3 %copy.9 = bf16[2048,256]{1,0:T(8,128)(2,1)} copy(bf16[2048,256]{1,0:T(8,128)(2,1)} %shard_map.73) | data formatting | bytes 2097152

commit v6 on v5

--- a/solution.py
+++ b/solution.py
@@ -9,7 +9,7 @@
 F32, BF16, I32 = jnp.float32, jnp.bfloat16, jnp.int32
 D, HEAD, SPAN = 2048, 128, 512
 OWN = 256
-DIRECT = 1
+DIRECT = 2
 PARTS = 4
 PART = OWN // PARTS
 QUERY, KEY, VALUE = 0, 1, 2
@@ -449,14 +449,13 @@
     a_direct(0)
     normalize(3)
     send_tokens(3)
-    a1(1)
+    a_direct(1)
     b1(0)
     a1(2)
     send_weights(QUERY, (3, 2, 1, 0))
     send_gains()
     forward_tokens(0)
     keep_spans.extend(keeps(chip_first + j * SPAN, SPAN) for j in range(8))
-    a2(1)
     a2(2)
     a1(3)
     b2(0)

time: 98 us -> 98.3 us (level)
  no operation moved by 1% of the time
where the time goes in v6:
time: 98.3 us; the launch traced here: 97.5 us
  Pallas kernels  95.3 us (97%)
  local copies, waits for them, and re-layouts  2.26 us (2%)
    pallas_call x1, Pallas kernels, per_device(): pl.pallas_call(kernel, out_shape=jax.ShapeDtypeStruct((2048, 256), BF16),...  95.3 us
    unnamed x1, local copies, waits for them, and re-layouts  2.26 us

profile of v6, /device:TPU:1, one launch (start us, length us, event | category | flops | bytes accessed | tf_op | source)
XLA Modules:
  0.0 97.5 jit_solution(14218935056435937471)
XLA Ops:
  0.0 95.3 %shard_map.73 = bf16[2048,256]{1,0:T(8,128)(2,1)} custom-call(bf16[256,2048]{1,0:T(8,128)(2,1)} %tok_hbm.1, f32[1,2048]{1,0:T(1,128)} %bitcast.3, f32[1,2048]{1,0:T(1,128)} %bitcast.4, s32[256,2048]{1,0:T(8,128)} %mask_hbm.1, bf16[3,64,256]{2,1,0:T(8,128)(2,1)} %proj_hbm.1, f32[1,256]{1,0:T(1,128)} %bitcast.5, s32[8]{0:T(128)} %traj_hbm.1), custom_call_target="tpu_custom_call" | custom-call | tf_op jit(solution)/shard_map/pallas_call | solution.py:587
  95.3 2.3 %copy.9 = bf16[2048,256]{1,0:T(8,128)(2,1)} copy(bf16[2048,256]{1,0:T(8,128)(2,1)} %shard_map.73) | data formatting | bytes 2097152
